TPU v7x, 32 devices: a whole 2x2x4 slice. The times are simulated.
32 devices in a mesh: gz: 8 (over y, x, core), xy: 4 (over z).
Axes of the slice: x: 2, y: 2, z: 4, core: 2. Of those that a mesh axis runs over, the one named last changes fastest.
Arguments:
- raw_volume: bfloat16 [16, 512, 512], P('gz', 'xy'), may hold values from -6 to 6
- weight_first: bfloat16 [32, 1, 3, 3], replicated, may hold values from -3 to 3
- bias_first: float32 [32], replicated, may hold values from -3 to 3
- weight_second: bfloat16 [64, 32, 3, 3], replicated, may hold values from -0.5 to 0.5
- bias_second: float32 [64], replicated, may hold values from -3 to 3
- weight_third: bfloat16 [128, 64, 3, 3], replicated, may hold values from -0.375 to 0.375
- bias_third: float32 [128], replicated, may hold values from -3 to 3
- weight_iso_a: bfloat16 [3, 3, 3, 128, 256], replicated, may hold values from -0.15625 to 0.15625
- bias_iso_a: float32 [256], replicated, may hold values from -3 to 3
- weight_iso_b: bfloat16 [3, 3, 3, 256, 256], replicated, may hold values from -0.109375 to 0.109375
- bias_iso_b: float32 [256], replicated, may hold values from -3 to 3
Outputs:
- features: bfloat16 [16, 64, 64, 256], P(None, 'xy', 'gz')
All inputs are finite; a program needn't handle non-finite values.
Results may differ from a plain program's by a relative error of at most 0.0069.
Values may be sent and summed in bfloat16 or wider, within the bound.
No kernel may reach another device: no remote copies, remote signals or barrier semaphores. Data moves between devices by JAX's collectives and lax.ppermute only.
A program may use at most 128 MiB of HBM per device.

v0:
```python
import functools

import jax
import jax.numpy as jnp
from jax import lax
from jax.experimental import pallas as pl
from jax.experimental.pallas import tpu as pltpu
from jax.sharding import PartitionSpec as P

HALO = 24
VMEM = pl.BlockSpec(memory_space=pltpu.VMEM)
F32 = jnp.float32
BF16 = jnp.bfloat16


def lane_iota(shape):
    return lax.broadcasted_iota(jnp.int32, shape, len(shape) - 1)


def shift_rows(x, down):
    sub = lax.broadcasted_iota(jnp.int32, x.shape, 2)
    if down:
        rolled = pltpu.roll(x, 1, 2)
        other = jnp.concatenate([rolled[:, -1:], rolled[:, :-1]], axis=1)
        return jnp.where(sub == 0, other, rolled)
    rolled = pltpu.roll(x, 7, 2)
    other = jnp.concatenate([rolled[:, 1:], rolled[:, :1]], axis=1)
    return jnp.where(sub == 7, other, rolled)


def tile_lanes(ref, row):
    x = ref[row : row + 1, :]
    return x + pltpu.roll(x, 32, 1) + pltpu.roll(x, 64, 1) + pltpu.roll(x, 96, 1)


def plane_kernel(
    cfg, lo, raw, hi, w1, b1, w2, b2, w3, b3, out,
    rs, small, t1, t2, t3, dd, ff, ppe, ppo,
):
    zl, rows, width, dests, vb = cfg
    third_rows = rows // 8
    tiles = third_rows // 8 + 1
    period = tiles * 8
    m = zl * period
    groups = width // 16 + 1
    first = lax.axis_index("xy") == 0
    last = lax.axis_index("xy") == lax.axis_size("xy") - 1
    sub8 = lax.broadcasted_iota(jnp.int32, (1, 1, 8, 128), 2)
    keep = jnp.where(sub8 < 4, jnp.where(last, 0.0, 1.0), jnp.where(first, 0.0, 1.0))

    def masked(x):
        n, lanes = x.shape
        x = x.reshape(n // period, tiles, 8, lanes)
        k = jnp.concatenate([keep] * (lanes // 128), axis=3)
        return jnp.concatenate([x[:, :-1], x[:, -1:] * k], axis=1)

    for z in range(zl):
        lo32 = lo[z].astype(F32)
        raw32 = raw[z].astype(F32)
        end = 8 + 8 * period
        rs[z, 0] = jnp.zeros((end + 8, 128), F32)
        rs[z, width // 128 + 1] = jnp.zeros((end + 8, 128), F32)
        hi32 = hi[z].astype(F32)
        for t in range(width // 128):
            cols = slice(128 * t, 128 * t + 128)
            rs[z, t + 1, 0:8] = lo32[HALO - 8 :, cols]
            rs[z, t + 1, 8 : 8 + rows] = raw32[:, cols]
            rs[z, t + 1, 8 + rows : 8 + rows + HALO] = hi32[:, cols]
            rs[z, t + 1, 8 + rows + HALO : end - HALO] = jnp.zeros((8 * period - rows - 2 * HALO, 128), F32)
            rs[z, t + 1, end - HALO : end] = lo32[:, cols]
            rs[z, t + 1, end : end + 8] = raw32[0:8, cols]

    small[...] = jnp.zeros_like(small)
    for ky in range(3):
        small[3 * ky : 3 * ky + 3, 0:32] = w1[ky].astype(F32)
    small[9:10, 0:32] = b1[...]
    small[10:11, 0:64] = b2[...]
    tap = []
    for i in range(10):
        x = tile_lanes(small, i)
        tap.append(jnp.concatenate([x, x], axis=1))
    bias1 = tap[9]
    x = small[10:11, :]
    bias2 = x + pltpu.roll(x, 64, 1)
    bias3 = b3[...]
    t1[...] = jnp.zeros_like(t1)
    gap = lax.broadcasted_iota(jnp.int32, (32, 256), 0) - 2 * (lane_iota((32, 256)) // 32)
    for ky in range(3):
        for dx in range(2):
            band = jnp.zeros((32, 256), F32)
            for kx in range(3):
                band = jnp.where(gap == dx + kx, tap[3 * ky + kx], band)
            band = band.astype(BF16)
            for dy in range(2):
                phase = 2 * dy + dx
                t1[64 * (ky + dy) : 64 * (ky + dy) + 32, 256 * phase : 256 * phase + 256] = band

    t2[...] = jnp.zeros_like(t2)
    t3[...] = jnp.zeros_like(t3)
    for ky in range(3):
        for kx in range(3):
            w = w2[ky, kx]
            for dy in range(2):
                for dx in range(2):
                    r, c = ky + dy, kx + dx
                    lanes = slice(128 * dy + 64 * dx, 128 * dy + 64 * dx + 64)
                    t2[0, 128 * r + 32 * c : 128 * r + 32 * c + 32, lanes] = w
                    c = (c + 2) % 4
                    t2[1, 128 * r + 32 * c : 128 * r + 32 * c + 32, lanes] = w
            w = w3[ky, kx]
            for dx in range(2):
                at = 256 * ky + 64 * (kx + dx)
                t3[at : at + 64, 128 * dx : 128 * dx + 128] = w

    lane = lane_iota((period, 128))
    for g in range(groups):
        start = 16 * g + 125
        t, s = start // 128, start % 128
        left = 128 - s
        for z in range(zl):
            for k in range(5):
                def piece(phase, tile, amount):
                    x = rs[z, tile, pl.ds(8 + phase, period, stride=8), :]
                    return pltpu.roll(x, amount % 128, 1)

                a = piece(2 * k - 1, t, -s)
                b = piece(2 * k, t, 64 - s)
                if left < 18:
                    a = jnp.where(lane < left, a, piece(2 * k - 1, t + 1, -s))
                    b = jnp.where(lane < 64 + left, b, piece(2 * k, t + 1, 64 - s))
                dd[k, g * m + z * period : g * m + z * period + period, :] = jnp.where(lane < 64, a, b).astype(BF16)

    chunk = 11 if groups % 11 == 0 else 1
    n = chunk * m
    for m1 in range(4):
        def level1(c, _, m1=m1):
            at = pl.multiple_of(c * n, 16)
            x = jnp.concatenate([dd[m1, pl.ds(at, n), :], dd[m1 + 1, pl.ds(at, n), :]], axis=1)
            acc = None
            for phase in range(4):
                y = jnp.dot(x, t1[:, 256 * phase : 256 * phase + 256], preferred_element_type=F32)
                acc = y if acc is None else jnp.maximum(acc, y)
            y = masked(jnp.maximum(acc + bias1, 0.0))
            row = pl.multiple_of(m + c * n, 16)
            ff[m1 + 1, pl.ds(row, n), :] = y.reshape(n, 256).astype(BF16)
            if m1 == 0:
                ff[5, pl.ds(row, n), :] = shift_rows(y, False).reshape(n, 256).astype(BF16)
            if m1 == 3:
                ff[0, pl.ds(row, n), :] = shift_rows(y, True).reshape(n, 256).astype(BF16)
            return 0

        lax.fori_loop(0, groups // chunk, level1, 0)
    for f in range(6):
        ff[f, 0:m, :] = jnp.zeros((m, 256), BF16)
        x = ff[f, m : 2 * m, 0:128].astype(F32)
        ff[f, m : 2 * m, 0:128] = jnp.where(lane_iota((m, 128)) < 32, 0.0, x).astype(BF16)
        x = ff[f, groups * m : (groups + 1) * m, 0:128].astype(F32)
        ff[f, groups * m : (groups + 1) * m, 0:128] = jnp.where(lane_iota((m, 128)) < 32, x, 0.0).astype(BF16)
        ff[f, groups * m : (groups + 1) * m, 128:256] = jnp.zeros((m, 128), BF16)

    def half(f, at, n, lanes):
        return ff[f, pl.ds(pl.multiple_of(at, 16), n), lanes : lanes + 128]

    def swapped(f, at_low, low, at_high, high, n):
        mask = lane_iota((n, 128)) < 64
        return jnp.where(mask, half(f, at_low, n, low), half(f, at_high, n, high))

    def level2(m2, at, n, even):
        low, high = [], []
        for r in range(4):
            f = 2 * m2 + r
            if even:
                low.append(swapped(f, at, 0, at - m, 128, n))
                high.append(half(f, at, n, 0))
            else:
                low.append(swapped(f, at, 128, at, 0, n))
                high.append(half(f, at, n, 128))
        low = jnp.dot(jnp.concatenate(low, axis=1), t2[1], preferred_element_type=F32)
        high = jnp.dot(jnp.concatenate(high, axis=1), t2[0], preferred_element_type=F32)
        low = jnp.maximum(low[:, :128], low[:, 128:])
        high = jnp.maximum(high[:, :128], high[:, 128:])
        mask = lane_iota((n, 128)) < 64
        y = jnp.maximum(jnp.where(mask, low, high), pltpu.roll(jnp.where(mask, high, low), 64, 1))
        return masked(jnp.maximum(y + bias2, 0.0))

    for even, pp, count in ((True, ppe, groups), (False, ppo, groups - 1)):
        chunk = 11 if count % 11 == 0 else 8 if count % 8 == 0 else 1
        n = chunk * m
        for m2 in range(2):
            def step(c, _, m2=m2, even=even, pp=pp, n=n):
                at = pl.multiple_of(c * n, 16)
                y = level2(m2, at + m, n, even)
                pp[m2 + 1, pl.ds(at, n), :] = y.reshape(n, 128).astype(BF16)
                if m2 == 0:
                    pp[3, pl.ds(at, n), :] = shift_rows(y, False).reshape(n, 128).astype(BF16)
                else:
                    pp[0, pl.ds(at, n), :] = shift_rows(y, True).reshape(n, 128).astype(BF16)
                return 0

            lax.fori_loop(0, count // chunk, step, 0)
    for s in range(4):
        x = ppe[s, 0:m, :].astype(F32)
        ppe[s, 0:m, :] = jnp.where(lane_iota((m, 128)) < 64, 0.0, x).astype(BF16)
        at = (groups - 1) * m
        x = ppe[s, at : at + m, :].astype(F32)
        ppe[s, at : at + m, :] = jnp.where(lane_iota((m, 128)) < 64, x, 0.0).astype(BF16)

    def level3(at, n, odd):
        acc = None
        for dy in range(2):
            x = []
            for r in range(3):
                here = pl.ds(pl.multiple_of(at, 16), n)
                after = pl.ds(pl.multiple_of(at + m, 16), n)
                x += [ppo[dy + r, here, :], ppe[dy + r, after, :]] if odd else [ppe[dy + r, here, :], ppo[dy + r, here, :]]
            y = jnp.dot(jnp.concatenate(x, axis=1), t3[...], preferred_element_type=F32)
            y = jnp.maximum(y[:, :128], y[:, 128:])
            acc = y if acc is None else jnp.maximum(acc, y)
        y = masked(jnp.maximum(acc + bias3, 0.0))
        return y.reshape(n // m, zl, tiles, 8, 128)

    zero = jnp.zeros((2 * (tiles - 1) + 1, zl * 8, 128), BF16)
    out[0, 0] = zero
    out[dests - 1, vb + 1] = zero
    chunk = 8
    n = chunk * m
    for c in range((groups - 1) // chunk):
        ys = [level3(c * n, n, odd) for odd in (False, True)]
        a, b = [y[:, :, tiles - 1].reshape(chunk * zl, 8, 128) for y in ys]
        sub = lax.broadcasted_iota(jnp.int32, a.shape, 1)
        edge = jnp.where(sub < 4, pltpu.roll(a, 2, 1), pltpu.roll(b, 6, 1))
        edge = edge.reshape(chunk, zl * 8, 128).astype(BF16)
        mains = [y[:, :, i].reshape(chunk, zl * 8, 128).astype(BF16) for y in ys for i in range(tiles - 1)]
        for w in range(chunk):
            v = c * chunk + w
            for d in range(dests):
                at = v - (vb * d - 1)
                if 0 <= at < vb + 2:
                    for i, part in enumerate(mains + [edge]):
                        out[d, at, i] = part[w]


def cube_kernel(cfg, recv, wa, ba, wb, bb, out, wav, wbv, a3, b3, sems):
    sources, zl, third_rows, vb, in_chan, mid_chan, out_chan, flip = cfg
    depth = sources * zl
    xs = 2 * vb
    tiles = third_rows // 8
    copy_a = pltpu.make_async_copy(wa, wav, sems.at[0])
    copy_b = pltpu.make_async_copy(wb, wbv, sems.at[1])
    copy_a.start()
    copy_b.start()

    rows = 8 * depth
    shape = (rows, rows)
    to = lax.broadcasted_iota(jnp.int32, shape, 0)
    at = lax.broadcasted_iota(jnp.int32, shape, 1)
    k_to, z_to = to // depth, to % depth
    k_at, z_at = at % 8, (at // (8 * zl)) * zl + (at // 8) % zl
    gather = jnp.concatenate(
        [jnp.where((k_to == k_at) & (z_at == z_to + dz), 1.0, 0.0).astype(BF16) for dz in (-1, 0, 1)], axis=0
    )
    parts = 2 * tiles + 1
    for vl in range(vb + 2):
        for c in range(parts):
            x = recv[:, vl, c].reshape(rows, in_chan)
            y = jnp.dot(gather, x, preferred_element_type=F32).astype(BF16).reshape(3, 8, depth, in_chan)
            for dz in range(3):
                lanes = slice(dz * in_chan, (dz + 1) * in_chan)
                if c < 2 * tiles:
                    x_at, y_at = 2 * vl + c // tiles, 2 + 8 * (c % tiles)
                    a3[y_at : y_at + 8, x_at, :, lanes] = y[dz]
                else:
                    for side in range(2):
                        a3[0:2, 2 * vl + side, :, lanes] = y[dz, 4 * side : 4 * side + 2]
                        a3[third_rows + 2 : third_rows + 4, 2 * vl + side, :, lanes] = y[dz, 4 * side + 2 : 4 * side + 4]

    copy_a.wait()
    taps = [(ky, kx) for ky in range(3) for kx in range(3)]
    mid_x = xs + 2
    mid_rows = third_rows + 2
    step_rows = 9 if mid_rows % 9 == 0 else 1

    def iso_a(c, _):
        y0 = c * step_rows
        n = step_rows * mid_x * depth
        x = jnp.concatenate(
            [a3[pl.ds(y0 + ky, step_rows), kx : kx + mid_x].reshape(n, 3 * in_chan) for ky, kx in taps], axis=1
        )
        w = jnp.concatenate([wav[dz, ky, kx] for ky, kx in taps for dz in range(3)], axis=0)
        y = jnp.dot(x, w, preferred_element_type=F32)
        y = jnp.maximum(y + ba[...], 0.0)
        here = (step_rows, mid_x, depth, mid_chan)
        b3[pl.ds(y0, step_rows), :, :, mid_chan : 2 * mid_chan] = y.reshape(here).astype(BF16)
        y = y.reshape(step_rows * mid_x, depth // 8, 8, mid_chan)
        sub = lax.broadcasted_iota(jnp.int32, y.shape, 2)
        none = jnp.zeros_like(y[:, :1])
        rolled = pltpu.roll(y, 1, 2)
        other = jnp.concatenate([none, rolled[:, :-1]], axis=1)
        down = jnp.where(sub == 0, other, rolled)
        b3[pl.ds(y0, step_rows), :, :, 0:mid_chan] = down.reshape(here).astype(BF16)
        rolled = pltpu.roll(y, 7, 2)
        other = jnp.concatenate([rolled[:, 1:], none], axis=1)
        up = jnp.where(sub == 7, other, rolled)
        b3[pl.ds(y0, step_rows), :, :, 2 * mid_chan : 3 * mid_chan] = up.reshape(here).astype(BF16)
        return 0

    lax.fori_loop(0, mid_rows // step_rows, iso_a, 0)

    row, col = lax.axis_index("xy"), lax.axis_index("gz")

    @pl.when(row == 0)
    def _():
        b3[0] = jnp.zeros(b3.shape[1:], BF16)

    @pl.when(row == lax.axis_size("xy") - 1)
    def _():
        b3[mid_rows - 1] = jnp.zeros(b3.shape[1:], BF16)

    @pl.when(col == 0)
    def _():
        b3[:, 0] = jnp.zeros((mid_rows,) + b3.shape[2:], BF16)

    @pl.when(col == lax.axis_size("gz") - 1)
    def _():
        b3[:, mid_x - 1] = jnp.zeros((mid_rows,) + b3.shape[2:], BF16)

    copy_b.wait()
    if flip:
        n = xs * depth
        to = lax.broadcasted_iota(jnp.int32, (n, n), 0)
        at = lax.broadcasted_iota(jnp.int32, (n, n), 1)
        turn = jnp.where((to // xs == at % depth) & (to % xs == at // depth), 1.0, 0.0).astype(BF16)
    out_rows = 8

    def iso_b(c, _):
        y0 = c * out_rows
        n = out_rows * xs * depth
        x = jnp.concatenate(
            [b3[pl.ds(y0 + ky, out_rows), kx : kx + xs].reshape(n, 3 * mid_chan) for ky, kx in taps], axis=1
        )
        w = jnp.concatenate([wbv[dz, ky, kx] for ky, kx in taps for dz in range(3)], axis=0)
        y = jnp.dot(x, w, preferred_element_type=F32)
        y = jnp.maximum(y + bb[...], 0.0).astype(BF16)
        if flip:
            y = y.reshape(out_rows, xs * depth, out_chan)
            for i in range(out_rows):
                t = jnp.dot(turn, y[i], preferred_element_type=F32).astype(BF16)
                out[:, y0 + i] = t.reshape(depth, xs, out_chan)
        else:
            out[pl.ds(y0, out_rows)] = y.reshape(out_rows, xs, depth, out_chan)
        return 0

    lax.fori_loop(0, third_rows // out_rows, iso_b, 0)


def body(
    raw_volume,
    weight_first,
    bias_first,
    weight_second,
    bias_second,
    weight_third,
    bias_third,
    weight_iso_a,
    bias_iso_a,
    weight_iso_b,
    bias_iso_b,
):
    zl, rows, width = raw_volume.shape
    dests = lax.axis_size("gz")
    depth = zl * dests
    third_rows = rows // 8
    vb = width // 8 // dests // 2
    count = lax.axis_size("xy")
    forward = [(i, i + 1) for i in range(count - 1)]
    backward = [(i + 1, i) for i in range(count - 1)]
    lo = lax.ppermute(raw_volume[:, rows - HALO :], "xy", forward)
    hi = lax.ppermute(raw_volume[:, :HALO], "xy", backward)

    period = third_rows + 8
    m = zl * period
    groups = width // 16 + 1
    parts = 2 * (third_rows // 8) + 1
    send = pl.pallas_call(
        functools.partial(plane_kernel, (zl, rows, width, dests, vb)),
        out_shape=jax.ShapeDtypeStruct((dests, vb + 2, parts, zl * 8, 128), BF16),
        in_specs=[VMEM] * 9,
        out_specs=VMEM,
        scratch_shapes=[
            pltpu.VMEM((zl, width // 128 + 2, 8 * period + 16, 128), F32),
            pltpu.VMEM((16, 128), F32),
            pltpu.VMEM((256, 1024), BF16),
            pltpu.VMEM((2, 512, 256), BF16),
            pltpu.VMEM((768, 256), BF16),
            pltpu.VMEM((5, groups * m, 128), BF16),
            pltpu.VMEM((6, (groups + 1) * m, 256), BF16),
            pltpu.VMEM((4, groups * m, 128), BF16),
            pltpu.VMEM((4, (groups - 1) * m, 128), BF16),
        ],
        compiler_params=pltpu.CompilerParams(vmem_limit_bytes=60 << 20),
        name="planes",
    )(
        lo, raw_volume, hi,
        jnp.transpose(weight_first, (1, 2, 3, 0))[0], bias_first[None],
        jnp.transpose(weight_second, (2, 3, 1, 0)), bias_second[None],
        jnp.transpose(weight_third, (2, 3, 1, 0)), bias_third[None],
    )
    recv = lax.all_to_all(send, "gz", split_axis=0, concat_axis=0, tiled=True)

    xs = 2 * vb
    in_chan, mid_chan = weight_iso_a.shape[3:]
    out_chan = weight_iso_b.shape[4]
    flip = xs % 8 == 0
    shape = (depth, third_rows, xs, out_chan) if flip else (third_rows, xs, depth, out_chan)
    anywhere = pl.BlockSpec(memory_space=pl.ANY)
    out = pl.pallas_call(
        functools.partial(cube_kernel, (dests, zl, third_rows, vb, in_chan, mid_chan, out_chan, flip)),
        out_shape=jax.ShapeDtypeStruct(shape, BF16),
        in_specs=[VMEM, anywhere, VMEM, anywhere, VMEM],
        out_specs=VMEM,
        scratch_shapes=[
            pltpu.VMEM(weight_iso_a.shape, BF16),
            pltpu.VMEM(weight_iso_b.shape, BF16),
            pltpu.VMEM((third_rows + 4, xs + 4, depth, 3 * in_chan), BF16),
            pltpu.VMEM((third_rows + 2, xs + 2, depth, 3 * mid_chan), BF16),
            pltpu.SemaphoreType.DMA((2,)),
        ],
        compiler_params=pltpu.CompilerParams(vmem_limit_bytes=60 << 20),
        name="cubes",
    )(recv, weight_iso_a, bias_iso_a[None], weight_iso_b, bias_iso_b[None])
    return out if flip else jnp.transpose(out, (2, 0, 1, 3))


def solution(mesh):
    placed = (P("gz", "xy", None), P(), P(), P(), P(), P(), P(), P(), P(), P(), P())
    return jax.shard_map(
        body, mesh=mesh, in_specs=placed, out_specs=P(None, "xy", "gz", None), check_vma=False
    )
```

profile of v0, /device:TPU:0, one launch (start us, length us, event | category | flops | bytes accessed | tf_op | source)
XLA Modules:
  0.0 65.4 jit_solution(15894709569472070667)
XLA Ops:
  0.0 0.8 %fusion = (bf16[2,24,512]{2,1,0:T(8,128)(2,1)S(1)}, bf16[2,24,512]{2,1,0:T(8,128)(2,1)S(1)}) fusion(bf16[2,128,512]{2,1,0:T(8,128)(2,1)} %raw.1), kind=kLoop, calls=%fused_computation | loop fusion | bytes 196608 | tf_op jit(solution)/shard_map/slice | solution.py:378
  0.8 1.3 %collective-permute-start.1 = (bf16[2,24,512]{2,1,0:T(8,128)(2,1)S(1)}, bf16[2,24,512]{2,1,0:T(8,128)(2,1)S(1)}, u32[]{:S(2)}, u32[]{:S(2)}) collective-permute-start(bf16[2,24,512]{2,1,0:T(8,128)(2,1)S(1)} %get-tuple-element.5), channel_id=1, source_target_pairs={{1,0},{2,1},{3,2},{5,4},{6,5},{7,6},{9,8},{10,9},{11,10},{13,12},{... | collective-permute-start | bytes 147464 | tf_op jit(solution)/shard_map/ppermute | solution.py:378
  2.1 5.6 %collective-permute-start = (bf16[2,24,512]{2,1,0:T(8,128)(2,1)S(1)}, bf16[2,24,512]{2,1,0:T(8,128)(2,1)S(1)}, u32[]{:S(2)}, u32[]{:S(2)}) collective-permute-start(bf16[2,24,512]{2,1,0:T(8,128)(2,1)S(1)} %get-tuple-element.6), channel_id=1, source_target_pairs={{0,1},{1,2},{2,3},{4,5},{5,6},{6,7},{8,9},{9,10},{10,11},{12,13},{... | collective-permute-start | bytes 147464 | tf_op jit(solution)/shard_map/ppermute | solution.py:377
  7.7 0.1 collective-permute-done.1.hi
  7.8 0.0 copy-start
  7.8 1.6 %collective-permute-done.lo = bf16[2,24,512]{2,1,0:T(8,128)(2,1)S(1)} collective-permute-done((bf16[2,24,512]{2,1,0:T(8,128)(2,1)S(1)}, bf16[2,24,512]{2,1,0:T(8,128)(2,1)S(1)}, u32[]{:S(2)}, u32[]{:S(2)}) %collective-permute-start) | collective-permute-done | bytes 49184 | tf_op jit(solution)/shard_map/ppermute | solution.py:377
  9.4 0.0 copy-start.1
  9.4 0.0 copy-done
  9.4 0.6 copy-done.1
  10.0 18.5 %planes.1 = bf16[8,6,5,16,128]{4,3,2,1,0:T(8,128)(2,1)} custom-call(bf16[2,24,512]{2,1,0:T(8,128)(2,1)} %copy-done.1, bf16[2,128,512]{2,1,0:T(8,128)(2,1)} %raw.1, bf16[2,24,512]{2,1,0:T(8,128)(2,1)} %copy-done, bf16[3,3,32]{2,1,0:T(4,128)(2,1)} %bitcast.12, f32[1,32]{1,0:T(1,128)} %bitcast.15, bf16[3,3,32,64]{3,2,1,0:T(8,128)(2,1)} %bitcast.11, ...), custom_call_target="tpu_custom_call" | custom-call | tf_op jit(solution)/shard_map/planes/pallas_call | solution.py:384
  28.5 18.9 %all_to_all.5.recv = bf16[8,6,5,16,128]{4,3,2,1,0:T(8,128)(2,1)} all-to-all(bf16[8,6,5,16,128]{4,3,2,1,0:T(8,128)(2,1)} %planes.1), channel_id=1, replica_groups=mesh['gz'=8,'xy'=4] {'gz'}, dimensions={0} | all-to-all | bytes 1966080 | tf_op jit(solution)/shard_map/all_to_all | solution.py:408
  47.4 17.9 %cubes.1 = bf16[16,16,8,256]{3,2,1,0:T(8,128)(2,1)} custom-call(bf16[8,6,5,16,128]{4,3,2,1,0:T(8,128)(2,1)} %all_to_all.5.recv, bf16[3,3,3,128,256]{4,3,2,1,0:T(8,128)(2,1)} %wa.1, f32[1,256]{1,0:T(1,128)} %bitcast.13, bf16[3,3,3,256,256]{4,3,2,1,0:T(8,128)(2,1)} %wb.1, f32[1,256]{1,0:T(1,128)} %bitcast.14), custom_call_target="tpu_custom_call" | custom-call | tf_op jit(solution)/shard_map/cubes/pallas_call | solution.py:416
Async XLA Ops:
  0.8 7.0 %collective-permute-start.1 = (bf16[2,24,512]{2,1,0:T(8,128)(2,1)S(1)}, bf16[2,24,512]{2,1,0:T(8,128)(2,1)S(1)}, u32[]{:S(2)}, u32[]{:S(2)}) collective-permute-start(bf16[2,24,512]{2,1,0:T(8,128)(2,1)S(1)} %get-tuple-element.5), channel_id=1, source_target_pairs={{1,0},{2,1},{3,2},{5,4},{6,5},{7,6},{9,8},{10,9},{11,10},{13,12},{... | collective-permute-start | bytes 147464 | tf_op jit(solution)/shard_map/ppermute | solution.py:378
  2.1 7.3 %collective-permute-start = (bf16[2,24,512]{2,1,0:T(8,128)(2,1)S(1)}, bf16[2,24,512]{2,1,0:T(8,128)(2,1)S(1)}, u32[]{:S(2)}, u32[]{:S(2)}) collective-permute-start(bf16[2,24,512]{2,1,0:T(8,128)(2,1)S(1)} %get-tuple-element.6), channel_id=1, source_target_pairs={{0,1},{1,2},{2,3},{4,5},{5,6},{6,7},{8,9},{9,10},{10,11},{12,13},{... | collective-permute-start | bytes 147464 | tf_op jit(solution)/shard_map/ppermute | solution.py:377
  7.8 1.6 %copy-start = (bf16[2,24,512]{2,1,0:T(8,128)(2,1)}, bf16[2,24,512]{2,1,0:T(8,128)(2,1)S(1)}, u32[]{:S(2)}) copy-start(bf16[2,24,512]{2,1,0:T(8,128)(2,1)S(1)} %collective-permute-done.1.hi) | copy-start | bytes 147460
  9.4 0.6 copy-start.1
where the time goes:
time: 65.7 us; the launch traced here: 65.4 us
  Pallas kernels  36.4 us (55%)
  blocking collectives  18.9 us (29%)
  starting transfers between devices  6.84 us (10%)
  waiting for transfers between devices  1.73 us (3%)
  local copies, waits for them, and re-layouts  1.44 us (2%)
    all_to_all x1, blocking collectives, body(): recv = lax.all_to_all(send, 'gz', split_axis=0, concat_axis=0, tiled=True)  18.9 us
    pallas_call x1, Pallas kernels, body(): pl.pallas_call(functools.partial(plane_kernel, (zl, rows, width, dests, v...  18.5 us
    pallas_call x1, Pallas kernels, body(): pl.pallas_call(functools.partial(cube_kernel, (dests, zl, third_rows, vb,...  17.9 us
    ppermute x1, starting transfers between devices, body(): lo = lax.ppermute(raw_volume[:, rows - HALO:], 'xy', forward)  5.56 us
    ppermute x1, waiting for transfers between devices, body(): lo = lax.ppermute(raw_volume[:, rows - HALO:], 'xy', forward)  1.6 us
  transfers between devices with their start and end apart: 2, of which 2 were waited for; matrix products, arithmetic and copies ran while one was open for 0% of the time, Pallas kernels for 0%

commit v1 on v0

--- a/solution.py
+++ b/solution.py
@@ -7,10 +7,16 @@
 from jax.experimental.pallas import tpu as pltpu
 from jax.sharding import PartitionSpec as P
 
+T2, T3, BIAS = 1024, 2048, 2816
 HALO = 24
 VMEM = pl.BlockSpec(memory_space=pltpu.VMEM)
 F32 = jnp.float32
 BF16 = jnp.bfloat16
+
+
+def unrolled(count, step):
+    for i in range(count):
+        step(i, 0)
 
 
 def lane_iota(shape):
@@ -33,9 +39,57 @@
     return x + pltpu.roll(x, 32, 1) + pltpu.roll(x, 64, 1) + pltpu.roll(x, 96, 1)
 
 
+def weight_kernel(w1, b1, w2, b2, w3, b3, banded, small):
+    small[...] = jnp.zeros_like(small)
+    for ky in range(3):
+        small[3 * ky : 3 * ky + 3, 0:32] = w1[ky].astype(F32)
+    small[9:10, 0:32] = b1[...]
+    small[10:11, 0:64] = b2[...]
+    tap = []
+    for i in range(10):
+        x = tile_lanes(small, i)
+        tap.append(jnp.concatenate([x, x], axis=1))
+    banded[...] = jnp.zeros_like(banded)
+    x = small[10:11, :]
+    x = x + pltpu.roll(x, 64, 1)
+    row = lax.broadcasted_iota(jnp.int32, (16, 256), 0)
+    rest = jnp.where(row < 3, tap[9], jnp.where(row < 6, jnp.concatenate([x, x], axis=1), jnp.concatenate([b3[...]] * 2, axis=1)))
+    high = rest.astype(BF16).astype(F32)
+    mid = (rest - high).astype(BF16).astype(F32)
+    low = rest - high - mid
+    banded[BIAS : BIAS + 16, :] = jnp.where(row % 3 == 0, high, jnp.where(row % 3 == 1, mid, low)).astype(BF16)
+    gap = lax.broadcasted_iota(jnp.int32, (32, 256), 0) - 2 * (lane_iota((32, 256)) // 32)
+    for ky in range(3):
+        for dx in range(2):
+            band = jnp.zeros((32, 256), F32)
+            for kx in range(3):
+                band = jnp.where(gap == dx + kx, tap[3 * ky + kx], band)
+            band = band.astype(BF16)
+            for dy in range(2):
+                phase = 2 * dy + dx
+                at = 256 * phase + 64 * (ky + dy)
+                banded[at : at + 32, :] = band
+
+    for ky in range(3):
+        for kx in range(3):
+            w = w2[ky, kx]
+            for dy in range(2):
+                for dx in range(2):
+                    r, c = ky + dy, kx + dx
+                    lanes = slice(128 * dy + 64 * dx, 128 * dy + 64 * dx + 64)
+                    at = T2 + 128 * r + 32 * c
+                    banded[at : at + 32, lanes] = w
+                    at = T2 + 512 + 128 * r + 32 * ((c + 2) % 4)
+                    banded[at : at + 32, lanes] = w
+            w = w3[ky, kx]
+            for dx in range(2):
+                at = T3 + 256 * ky + 64 * (kx + dx)
+                banded[at : at + 64, 128 * dx : 128 * dx + 128] = w
+
+
 def plane_kernel(
-    cfg, lo, raw, hi, w1, b1, w2, b2, w3, b3, out,
-    rs, small, t1, t2, t3, dd, ff, ppe, ppo,
+    cfg, swap_a, raw, swap_b, banded, out,
+    rs, dd, ff, ppe, ppo,
 ):
     zl, rows, width, dests, vb = cfg
     third_rows = rows // 8
@@ -45,6 +99,7 @@
     groups = width // 16 + 1
     first = lax.axis_index("xy") == 0
     last = lax.axis_index("xy") == lax.axis_size("xy") - 1
+    even = lax.axis_index("xy") % 2 == 0
     sub8 = lax.broadcasted_iota(jnp.int32, (1, 1, 8, 128), 2)
     keep = jnp.where(sub8 < 4, jnp.where(last, 0.0, 1.0), jnp.where(first, 0.0, 1.0))
 
@@ -55,12 +110,12 @@
         return jnp.concatenate([x[:, :-1], x[:, -1:] * k], axis=1)
 
     for z in range(zl):
-        lo32 = lo[z].astype(F32)
+        a32, b32 = swap_a[z].astype(F32), swap_b[z].astype(F32)
+        lo32, hi32 = jnp.where(even, b32, a32), jnp.where(even, a32, b32)
         raw32 = raw[z].astype(F32)
         end = 8 + 8 * period
         rs[z, 0] = jnp.zeros((end + 8, 128), F32)
         rs[z, width // 128 + 1] = jnp.zeros((end + 8, 128), F32)
-        hi32 = hi[z].astype(F32)
         for t in range(width // 128):
             cols = slice(128 * t, 128 * t + 128)
             rs[z, t + 1, 0:8] = lo32[HALO - 8 :, cols]
@@ -69,48 +124,6 @@
             rs[z, t + 1, 8 + rows + HALO : end - HALO] = jnp.zeros((8 * period - rows - 2 * HALO, 128), F32)
             rs[z, t + 1, end - HALO : end] = lo32[:, cols]
             rs[z, t + 1, end : end + 8] = raw32[0:8, cols]
-
-    small[...] = jnp.zeros_like(small)
-    for ky in range(3):
-        small[3 * ky : 3 * ky + 3, 0:32] = w1[ky].astype(F32)
-    small[9:10, 0:32] = b1[...]
-    small[10:11, 0:64] = b2[...]
-    tap = []
-    for i in range(10):
-        x = tile_lanes(small, i)
-        tap.append(jnp.concatenate([x, x], axis=1))
-    bias1 = tap[9]
-    x = small[10:11, :]
-    bias2 = x + pltpu.roll(x, 64, 1)
-    bias3 = b3[...]
-    t1[...] = jnp.zeros_like(t1)
-    gap = lax.broadcasted_iota(jnp.int32, (32, 256), 0) - 2 * (lane_iota((32, 256)) // 32)
-    for ky in range(3):
-        for dx in range(2):
-            band = jnp.zeros((32, 256), F32)
-            for kx in range(3):
-                band = jnp.where(gap == dx + kx, tap[3 * ky + kx], band)
-            band = band.astype(BF16)
-            for dy in range(2):
-                phase = 2 * dy + dx
-                t1[64 * (ky + dy) : 64 * (ky + dy) + 32, 256 * phase : 256 * phase + 256] = band
-
-    t2[...] = jnp.zeros_like(t2)
-    t3[...] = jnp.zeros_like(t3)
-    for ky in range(3):
-        for kx in range(3):
-            w = w2[ky, kx]
-            for dy in range(2):
-                for dx in range(2):
-                    r, c = ky + dy, kx + dx
-                    lanes = slice(128 * dy + 64 * dx, 128 * dy + 64 * dx + 64)
-                    t2[0, 128 * r + 32 * c : 128 * r + 32 * c + 32, lanes] = w
-                    c = (c + 2) % 4
-                    t2[1, 128 * r + 32 * c : 128 * r + 32 * c + 32, lanes] = w
-            w = w3[ky, kx]
-            for dx in range(2):
-                at = 256 * ky + 64 * (kx + dx)
-                t3[at : at + 64, 128 * dx : 128 * dx + 128] = w
 
     lane = lane_iota((period, 128))
     for g in range(groups):
@@ -130,18 +143,21 @@
                     b = jnp.where(lane < 64 + left, b, piece(2 * k, t + 1, 64 - s))
                 dd[k, g * m + z * period : g * m + z * period + period, :] = jnp.where(lane < 64, a, b).astype(BF16)
 
+    bias = [sum(banded[BIAS + 3 * i + j : BIAS + 3 * i + j + 1, :].astype(F32) for j in range(3)) for i in range(3)]
+    bias1, bias2, bias3 = bias[0], bias[1][:, :128], bias[2][:, :128]
+
     chunk = 11 if groups % 11 == 0 else 1
     n = chunk * m
     for m1 in range(4):
         def level1(c, _, m1=m1):
-            at = pl.multiple_of(c * n, 16)
+            at = c * n
             x = jnp.concatenate([dd[m1, pl.ds(at, n), :], dd[m1 + 1, pl.ds(at, n), :]], axis=1)
             acc = None
             for phase in range(4):
-                y = jnp.dot(x, t1[:, 256 * phase : 256 * phase + 256], preferred_element_type=F32)
+                y = jnp.dot(x, banded[256 * phase : 256 * phase + 256, :], preferred_element_type=F32)
                 acc = y if acc is None else jnp.maximum(acc, y)
             y = masked(jnp.maximum(acc + bias1, 0.0))
-            row = pl.multiple_of(m + c * n, 16)
+            row = m + c * n
             ff[m1 + 1, pl.ds(row, n), :] = y.reshape(n, 256).astype(BF16)
             if m1 == 0:
                 ff[5, pl.ds(row, n), :] = shift_rows(y, False).reshape(n, 256).astype(BF16)
@@ -149,7 +165,7 @@
                 ff[0, pl.ds(row, n), :] = shift_rows(y, True).reshape(n, 256).astype(BF16)
             return 0
 
-        lax.fori_loop(0, groups // chunk, level1, 0)
+        unrolled(groups // chunk, level1)
     for f in range(6):
         ff[f, 0:m, :] = jnp.zeros((m, 256), BF16)
         x = ff[f, m : 2 * m, 0:128].astype(F32)
@@ -159,7 +175,7 @@
         ff[f, groups * m : (groups + 1) * m, 128:256] = jnp.zeros((m, 128), BF16)
 
     def half(f, at, n, lanes):
-        return ff[f, pl.ds(pl.multiple_of(at, 16), n), lanes : lanes + 128]
+        return ff[f, pl.ds(at, n), lanes : lanes + 128]
 
     def swapped(f, at_low, low, at_high, high, n):
         mask = lane_iota((n, 128)) < 64
@@ -175,8 +191,8 @@
             else:
                 low.append(swapped(f, at, 128, at, 0, n))
                 high.append(half(f, at, n, 128))
-        low = jnp.dot(jnp.concatenate(low, axis=1), t2[1], preferred_element_type=F32)
-        high = jnp.dot(jnp.concatenate(high, axis=1), t2[0], preferred_element_type=F32)
+        low = jnp.dot(jnp.concatenate(low, axis=1), banded[T2 + 512 : T2 + 1024, :], preferred_element_type=F32)
+        high = jnp.dot(jnp.concatenate(high, axis=1), banded[T2 : T2 + 512, :], preferred_element_type=F32)
         low = jnp.maximum(low[:, :128], low[:, 128:])
         high = jnp.maximum(high[:, :128], high[:, 128:])
         mask = lane_iota((n, 128)) < 64
@@ -188,7 +204,7 @@
         n = chunk * m
         for m2 in range(2):
             def step(c, _, m2=m2, even=even, pp=pp, n=n):
-                at = pl.multiple_of(c * n, 16)
+                at = c * n
                 y = level2(m2, at + m, n, even)
                 pp[m2 + 1, pl.ds(at, n), :] = y.reshape(n, 128).astype(BF16)
                 if m2 == 0:
@@ -197,7 +213,7 @@
                     pp[0, pl.ds(at, n), :] = shift_rows(y, True).reshape(n, 128).astype(BF16)
                 return 0
 
-            lax.fori_loop(0, count // chunk, step, 0)
+            unrolled(count // chunk, step)
     for s in range(4):
         x = ppe[s, 0:m, :].astype(F32)
         ppe[s, 0:m, :] = jnp.where(lane_iota((m, 128)) < 64, 0.0, x).astype(BF16)
@@ -210,10 +226,10 @@
         for dy in range(2):
             x = []
             for r in range(3):
-                here = pl.ds(pl.multiple_of(at, 16), n)
-                after = pl.ds(pl.multiple_of(at + m, 16), n)
+                here = pl.ds(at, n)
+                after = pl.ds(at + m, n)
                 x += [ppo[dy + r, here, :], ppe[dy + r, after, :]] if odd else [ppe[dy + r, here, :], ppo[dy + r, here, :]]
-            y = jnp.dot(jnp.concatenate(x, axis=1), t3[...], preferred_element_type=F32)
+            y = jnp.dot(jnp.concatenate(x, axis=1), banded[T3 : T3 + 768, :], preferred_element_type=F32)
             y = jnp.maximum(y[:, :128], y[:, 128:])
             acc = y if acc is None else jnp.maximum(acc, y)
         y = masked(jnp.maximum(acc + bias3, 0.0))
@@ -240,29 +256,30 @@
                         out[d, at, i] = part[w]
 
 
-def cube_kernel(cfg, recv, wa, ba, wb, bb, out, wav, wbv, a3, b3, sems):
+def cube_kernel(cfg, *refs):
     sources, zl, third_rows, vb, in_chan, mid_chan, out_chan, flip = cfg
+    near, far = refs[: sources // 2], refs[sources // 2 : sources]
+    wa, ba, wb, bb, out, a3, b3 = refs[sources:]
+    me = lax.axis_index("gz")
     depth = sources * zl
     xs = 2 * vb
     tiles = third_rows // 8
-    copy_a = pltpu.make_async_copy(wa, wav, sems.at[0])
-    copy_b = pltpu.make_async_copy(wb, wbv, sems.at[1])
-    copy_a.start()
-    copy_b.start()
 
     rows = 8 * depth
     shape = (rows, rows)
     to = lax.broadcasted_iota(jnp.int32, shape, 0)
     at = lax.broadcasted_iota(jnp.int32, shape, 1)
     k_to, z_to = to // depth, to % depth
-    k_at, z_at = at % 8, (at // (8 * zl)) * zl + (at // 8) % zl
+    k_at, z_at = at % 8, ((at // (8 * zl)) ^ me) * zl + (at // 8) % zl
     gather = jnp.concatenate(
         [jnp.where((k_to == k_at) & (z_at == z_to + dz), 1.0, 0.0).astype(BF16) for dz in (-1, 0, 1)], axis=0
     )
     parts = 2 * tiles + 1
     for vl in range(vb + 2):
         for c in range(parts):
-            x = recv[:, vl, c].reshape(rows, in_chan)
+            x = jnp.concatenate(
+                [part for k in range(sources // 2) for part in (near[k][(me % 2) * vb + vl, c], far[k][vl, c])], axis=0
+            )
             y = jnp.dot(gather, x, preferred_element_type=F32).astype(BF16).reshape(3, 8, depth, in_chan)
             for dz in range(3):
                 lanes = slice(dz * in_chan, (dz + 1) * in_chan)
@@ -274,7 +291,6 @@
                         a3[0:2, 2 * vl + side, :, lanes] = y[dz, 4 * side : 4 * side + 2]
                         a3[third_rows + 2 : third_rows + 4, 2 * vl + side, :, lanes] = y[dz, 4 * side + 2 : 4 * side + 4]
 
-    copy_a.wait()
     taps = [(ky, kx) for ky in range(3) for kx in range(3)]
     mid_x = xs + 2
     mid_rows = third_rows + 2
@@ -286,7 +302,7 @@
         x = jnp.concatenate(
             [a3[pl.ds(y0 + ky, step_rows), kx : kx + mid_x].reshape(n, 3 * in_chan) for ky, kx in taps], axis=1
         )
-        w = jnp.concatenate([wav[dz, ky, kx] for ky, kx in taps for dz in range(3)], axis=0)
+        w = jnp.concatenate([wa[dz, ky, kx] for ky, kx in taps for dz in range(3)], axis=0)
         y = jnp.dot(x, w, preferred_element_type=F32)
         y = jnp.maximum(y + ba[...], 0.0)
         here = (step_rows, mid_x, depth, mid_chan)
@@ -324,7 +340,6 @@
     def _():
         b3[:, mid_x - 1] = jnp.zeros((mid_rows,) + b3.shape[2:], BF16)
 
-    copy_b.wait()
     if flip:
         n = xs * depth
         to = lax.broadcasted_iota(jnp.int32, (n, n), 0)
@@ -338,7 +353,7 @@
         x = jnp.concatenate(
             [b3[pl.ds(y0 + ky, out_rows), kx : kx + xs].reshape(n, 3 * mid_chan) for ky, kx in taps], axis=1
         )
-        w = jnp.concatenate([wbv[dz, ky, kx] for ky, kx in taps for dz in range(3)], axis=0)
+        w = jnp.concatenate([wb[dz, ky, kx] for ky, kx in taps for dz in range(3)], axis=0)
         y = jnp.dot(x, w, preferred_element_type=F32)
         y = jnp.maximum(y + bb[...], 0.0).astype(BF16)
         if flip:
@@ -372,62 +387,77 @@
     third_rows = rows // 8
     vb = width // 8 // dests // 2
     count = lax.axis_size("xy")
-    forward = [(i, i + 1) for i in range(count - 1)]
-    backward = [(i + 1, i) for i in range(count - 1)]
-    lo = lax.ppermute(raw_volume[:, rows - HALO :], "xy", forward)
-    hi = lax.ppermute(raw_volume[:, :HALO], "xy", backward)
+    even = lax.axis_index("xy") % 2 == 0
+
+    def swap(start, pairs):
+        edge = lax.dynamic_slice_in_dim(raw_volume, start, HALO, axis=1)
+        return lax.ppermute(edge, "xy", [(i, i + 1) for i in pairs] + [(i + 1, i) for i in pairs])
+
+    first = swap(jnp.where(even, rows - HALO, 0), range(0, count - 1, 2))
+    second = swap(jnp.where(even, 0, rows - HALO), range(1, count - 1, 2))
 
     period = third_rows + 8
     m = zl * period
     groups = width // 16 + 1
     parts = 2 * (third_rows // 8) + 1
+    banded = pl.pallas_call(
+        weight_kernel,
+        out_shape=jax.ShapeDtypeStruct((BIAS + 16, 256), BF16),
+        in_specs=[VMEM] * 6,
+        out_specs=VMEM,
+        scratch_shapes=[pltpu.VMEM((16, 128), F32)],
+        compiler_params=pltpu.CompilerParams(vmem_limit_bytes=60 << 20),
+        cost_estimate=pl.CostEstimate(flops=2000000000, bytes_accessed=2000000, transcendentals=0),
+        name="weights",
+    )(
+        jnp.transpose(weight_first, (1, 2, 3, 0))[0], bias_first[None],
+        jnp.transpose(weight_second, (2, 3, 1, 0)), bias_second[None],
+        jnp.transpose(weight_third, (2, 3, 1, 0)), bias_third[None],
+    )
+    chips = dests // 2
     send = pl.pallas_call(
-        functools.partial(plane_kernel, (zl, rows, width, dests, vb)),
-        out_shape=jax.ShapeDtypeStruct((dests, vb + 2, parts, zl * 8, 128), BF16),
-        in_specs=[VMEM] * 9,
+        functools.partial(plane_kernel, (zl, rows, width, chips, 2 * vb)),
+        out_shape=jax.ShapeDtypeStruct((chips, 2 * vb + 2, parts, zl * 8, 128), BF16),
+        in_specs=[VMEM] * 4,
         out_specs=VMEM,
         scratch_shapes=[
             pltpu.VMEM((zl, width // 128 + 2, 8 * period + 16, 128), F32),
-            pltpu.VMEM((16, 128), F32),
-            pltpu.VMEM((256, 1024), BF16),
-            pltpu.VMEM((2, 512, 256), BF16),
-            pltpu.VMEM((768, 256), BF16),
             pltpu.VMEM((5, groups * m, 128), BF16),
             pltpu.VMEM((6, (groups + 1) * m, 256), BF16),
             pltpu.VMEM((4, groups * m, 128), BF16),
             pltpu.VMEM((4, (groups - 1) * m, 128), BF16),
         ],
-        compiler_params=pltpu.CompilerParams(vmem_limit_bytes=60 << 20),
+        compiler_params=pltpu.CompilerParams(vmem_limit_bytes=20 << 20),
         name="planes",
-    )(
-        lo, raw_volume, hi,
-        jnp.transpose(weight_first, (1, 2, 3, 0))[0], bias_first[None],
-        jnp.transpose(weight_second, (2, 3, 1, 0)), bias_second[None],
-        jnp.transpose(weight_third, (2, 3, 1, 0)), bias_third[None],
-    )
-    recv = lax.all_to_all(send, "gz", split_axis=0, concat_axis=0, tiled=True)
+    )(first, raw_volume, second, banded)
+    me = lax.axis_index("gz")
+    other = (1 - me % 2) * vb
+    near, far = [], []
+    for k in range(chips):
+        block = lax.dynamic_index_in_dim(send, (me // 2) ^ k, 0, keepdims=False)
+        if k:
+            block = lax.ppermute(block, "gz", [(i, i ^ (2 * k)) for i in range(dests)])
+        near.append(block)
+        window = lax.dynamic_slice_in_dim(block, other, vb + 2, axis=0)
+        far.append(lax.ppermute(window, "gz", [(i, i ^ 1) for i in range(dests)]))
 
     xs = 2 * vb
     in_chan, mid_chan = weight_iso_a.shape[3:]
     out_chan = weight_iso_b.shape[4]
     flip = xs % 8 == 0
     shape = (depth, third_rows, xs, out_chan) if flip else (third_rows, xs, depth, out_chan)
-    anywhere = pl.BlockSpec(memory_space=pl.ANY)
     out = pl.pallas_call(
         functools.partial(cube_kernel, (dests, zl, third_rows, vb, in_chan, mid_chan, out_chan, flip)),
         out_shape=jax.ShapeDtypeStruct(shape, BF16),
-        in_specs=[VMEM, anywhere, VMEM, anywhere, VMEM],
+        in_specs=[VMEM] * (dests + 4),
         out_specs=VMEM,
         scratch_shapes=[
-            pltpu.VMEM(weight_iso_a.shape, BF16),
-            pltpu.VMEM(weight_iso_b.shape, BF16),
             pltpu.VMEM((third_rows + 4, xs + 4, depth, 3 * in_chan), BF16),
             pltpu.VMEM((third_rows + 2, xs + 2, depth, 3 * mid_chan), BF16),
-            pltpu.SemaphoreType.DMA((2,)),
         ],
-        compiler_params=pltpu.CompilerParams(vmem_limit_bytes=60 << 20),
+        compiler_params=pltpu.CompilerParams(vmem_limit_bytes=(20 if depth <= 16 else 48) << 20),
         name="cubes",
-    )(recv, weight_iso_a, bias_iso_a[None], weight_iso_b, bias_iso_b[None])
+    )(*near, *far, weight_iso_a, bias_iso_a[None], weight_iso_b, bias_iso_b[None])
     return out if flip else jnp.transpose(out, (2, 0, 1, 3))
 
 

time: 65.7 us -> 53.8 us (0.82)
  the two profiles are of different devices: /device:TPU:0 before, /device:TPU:13 now
where the time goes in v1:
time: 53.8 us; the launch traced here: 53.5 us
  Pallas kernels  29.3 us (54%)
  starting transfers between devices  17 us (32%)
  local copies, waits for them, and re-layouts  5.08 us (9%)
  waiting for transfers between devices  2.03 us (4%)
    pallas_call x1, Pallas kernels, body(): pl.pallas_call(functools.partial(cube_kernel, (dests, zl, third_rows, vb,...  16.3 us
    pallas_call x1, Pallas kernels, body(): pl.pallas_call(functools.partial(plane_kernel, (zl, rows, width, chips, 2...  10.5 us
    ppermute x4, starting transfers between devices, body(): far.append(lax.ppermute(window, 'gz', [(i, i ^ 1) for i in range(dests)]))  9.86 us
    ppermute x2, starting transfers between devices, swap(): lax.ppermute(edge, 'xy', [(i, i + 1) for i in pairs] + [(i + 1, i) for i...  4.54 us
    unnamed x12, local copies, waits for them, and re-layouts  3.38 us
    ppermute x3, starting transfers between devices, body(): block = lax.ppermute(block, 'gz', [(i, i ^ 2 * k) for i in range(dests)])  2.65 us
    pallas_call x1, Pallas kernels, body(): pl.pallas_call(weight_kernel, out_shape=jax.ShapeDtypeStruct((BIAS + 16,...  2.45 us
    ppermute x4, waiting for transfers between devices, body(): far.append(lax.ppermute(window, 'gz', [(i, i ^ 1) for i in range(dests)]))  1.3 us
  transfers between devices with their start and end apart: 9, of which 3 were waited for; matrix products, arithmetic and copies ran while one was open for 0% of the time, Pallas kernels for 5%

profile of v1, /device:TPU:13, one launch (start us, length us, event | category | flops | bytes accessed | tf_op | source)
XLA Modules:
  0.0 53.5 jit_solution(16526820535411375238)
XLA Ops:
  0.0 0.8 %constant_dynamic-slice_fusion.3 = (bf16[2,24,512]{2,1,0:T(8,128)(2,1)S(1)}, bf16[2,24,512]{2,1,0:T(8,128)(2,1)S(1)}) fusion(bf16[2,128,512]{2,1,0:T(8,128)(2,1)} %raw.1, s32[]{:T(128)S(6)} %select_n.52, s32[]{:T(128)S(6)} %select_n.51), kind=kLoop, calls=%fused_computation.8 | loop fusion | bytes 196616 | tf_op jit(solution)/shard_map/dynamic_slice | solution.py:393
  0.8 0.2 collective-permute-start
  1.0 4.3 %collective-permute-start.1 = (bf16[2,24,512]{2,1,0:T(8,128)(2,1)S(1)}, bf16[2,24,512]{2,1,0:T(8,128)(2,1)S(1)}, u32[]{:S(2)}, u32[]{:S(2)}) collective-permute-start(bf16[2,24,512]{2,1,0:T(8,128)(2,1)S(1)} %get-tuple-element.9), channel_id=1, source_target_pairs={{1,2},{2,1},{5,6},{6,5},{9,10},{10,9},{13,14},{14,13},{17,18},{18,... | collective-permute-start | bytes 147464 | tf_op jit(solution)/shard_map/ppermute | solution.py:394
  5.4 0.0 copy-start.3
  5.4 2.4 %weights.1.banded = bf16[2832,256]{1,0:T(8,128)(2,1)} custom-call(bf16[3,3,32]{2,1,0:T(4,128)(2,1)} %bitcast.24, f32[1,32]{1,0:T(1,128)} %bitcast.25, bf16[3,3,32,64]{3,2,1,0:T(8,128)(2,1)} %bitcast.23, f32[1,64]{1,0:T(1,128)} %bitcast.26, bf16[3,3,64,128]{3,2,1,0:T(8,128)(2,1)} %bitcast.22, f32[1,128]{1,0:T(1,128)} %bitcast.27), custom_call_target="tpu_custom_call" | custom-call | flops 2000000000 | bytes 2000000 | tf_op jit(solution)/shard_map/weights/pallas_call | solution.py:403
  7.9 1.4 %copy-done.2 = bf16[2832,256]{1,0:T(8,128)(2,1)S(1)} copy-done((bf16[2832,256]{1,0:T(8,128)(2,1)S(1)}, bf16[2832,256]{1,0:T(8,128)(2,1)}, u32[]{:S(2)}) %copy-start.2) | copy-done | bytes 1450008
  9.2 10.5 %planes.1 = bf16[4,10,5,16,128]{4,3,2,1,0:T(8,128)(2,1)S(1)} custom-call(bf16[2,24,512]{2,1,0:T(8,128)(2,1)S(1)} %collective-permute-done.swap_a, bf16[2,128,512]{2,1,0:T(8,128)(2,1)S(1)} %copy-done.3, bf16[2,24,512]{2,1,0:T(8,128)(2,1)S(1)} %collective-permute-done.1.swap_b, bf16[2832,256]{1,0:T(8,128)(2,1)S(1)} %copy-done.2), custom_call_target="tpu_custom_call" | custom-call | tf_op jit(solution)/shard_map/planes/pallas_call | solution.py:418
  19.7 0.0 copy-start.1
  19.7 0.0 copy-start.4
  19.8 0.0 copy-start.5
  19.8 0.8 %dynamic-slice_bitcast_fusion = (bf16[10,5,16,128]{3,2,1,0:T(8,128)(2,1)S(1)}, bf16[10,5,16,128]{3,2,1,0:T(8,128)(2,1)S(1)}, bf16[10,5,16,128]{3,2,1,0:T(8,128)(2,1)}, bf16[10,5,16,128]{3,2,1,0:T(8,128)(2,1)S(1)}) fusion(bf16[4,10,5,16,128]{4,3,2,1,0:T(8,128)(2,1)S(1)} %planes.1, s32[]{:T(128)S(6)} %select_n.57, s32[]{:T(128)S(6)} %select_n.56, ...), kind=kLoop, calls=%fused_computation | loop fusion | bytes 1638416 | tf_op jit(solution)/shard_map/jit(dynamic_index_in_dim)/squeeze | solution.py:437
  20.6 1.2 %collective-permute-start.2 = (bf16[10,5,16,128]{3,2,1,0:T(8,128)(2,1)}, bf16[10,5,16,128]{3,2,1,0:T(8,128)(2,1)S(1)}, u32[]{:S(2)}, u32[]{:S(2)}) collective-permute-start(bf16[10,5,16,128]{3,2,1,0:T(8,128)(2,1)} %get-tuple-element.7), channel_id=1, source_target_pairs={{0,8},{4,12},{8,0},{12,4},{16,24},{20,28},{24,16},{28,20},{1,9},{5... | collective-permute-start | bytes 614408 | tf_op jit(solution)/shard_map/ppermute | solution.py:439
  21.8 0.2 collective-permute-start.3
  22.0 1.2 %collective-permute-start.4 = (bf16[10,5,16,128]{3,2,1,0:T(8,128)(2,1)S(1)}, bf16[10,5,16,128]{3,2,1,0:T(8,128)(2,1)S(1)}, u32[]{:S(2)}, u32[]{:S(2)}) collective-permute-start(bf16[10,5,16,128]{3,2,1,0:T(8,128)(2,1)S(1)} %get-tuple-element.5), channel_id=1, source_target_pairs={{0,24},{4,28},{8,16},{12,20},{16,8},{20,12},{24,0},{28,4},{1,25},{... | collective-permute-start | bytes 614408 | tf_op jit(solution)/shard_map/ppermute | solution.py:439
  23.3 2.2 %collective-permute-start.5 = (bf16[6,5,16,128]{3,2,1,0:T(8,128)(2,1)S(1)}, bf16[6,5,16,128]{3,2,1,0:T(8,128)(2,1)S(1)}, u32[]{:S(2)}, u32[]{:S(2)}) collective-permute-start(bf16[6,5,16,128]{3,2,1,0:T(8,128)(2,1)S(1)} %dynamic-slice_bitcast_fusion.4), channel_id=1, source_target_pairs={{0,4},{4,0},{8,12},{12,8},{16,20},{20,16},{24,28},{28,24},{1,5},{5... | collective-permute-start | bytes 368648 | tf_op jit(solution)/shard_map/ppermute | solution.py:442
  25.4 0.7 %collective-permute-done.2.refs_1_ = bf16[10,5,16,128]{3,2,1,0:T(8,128)(2,1)S(1)} collective-permute-done((bf16[10,5,16,128]{3,2,1,0:T(8,128)(2,1)}, bf16[10,5,16,128]{3,2,1,0:T(8,128)(2,1)S(1)}, u32[]{:S(2)}, u32[]{:S(2)}) %collective-permute-start.2) | collective-permute-done | bytes 204832 | tf_op jit(solution)/shard_map/ppermute | solution.py:439
  26.1 4.0 %collective-permute-start.6 = (bf16[6,5,16,128]{3,2,1,0:T(8,128)(2,1)S(1)}, bf16[6,5,16,128]{3,2,1,0:T(8,128)(2,1)S(1)}, u32[]{:S(2)}, u32[]{:S(2)}) collective-permute-start(bf16[6,5,16,128]{3,2,1,0:T(8,128)(2,1)S(1)} %constant_dynamic-slice_fusion.2), channel_id=1, source_target_pairs={{0,4},{4,0},{8,12},{12,8},{16,20},{20,16},{24,28},{28,24},{1,5},{5... | collective-permute-start | bytes 368648 | tf_op jit(solution)/shard_map/ppermute | solution.py:442
  30.2 3.6 %collective-permute-start.7 = (bf16[6,5,16,128]{3,2,1,0:T(8,128)(2,1)S(1)}, bf16[6,5,16,128]{3,2,1,0:T(8,128)(2,1)S(1)}, u32[]{:S(2)}, u32[]{:S(2)}) collective-permute-start(bf16[6,5,16,128]{3,2,1,0:T(8,128)(2,1)S(1)} %constant_dynamic-slice_fusion.1), channel_id=1, source_target_pairs={{0,4},{4,0},{8,12},{12,8},{16,20},{20,16},{24,28},{28,24},{1,5},{5... | collective-permute-start | bytes 368648 | tf_op jit(solution)/shard_map/ppermute | solution.py:442
  33.8 0.1 collective-permute-start.8
  33.9 0.9 %collective-permute-done.7.refs_6_ = bf16[6,5,16,128]{3,2,1,0:T(8,128)(2,1)S(1)} collective-permute-done((bf16[6,5,16,128]{3,2,1,0:T(8,128)(2,1)S(1)}, bf16[6,5,16,128]{3,2,1,0:T(8,128)(2,1)S(1)}, u32[]{:S(2)}, u32[]{:S(2)}) %collective-permute-start.7) | collective-permute-done | bytes 122912 | tf_op jit(solution)/shard_map/ppermute | solution.py:442
  34.7 0.4 collective-permute-done.8.refs_7_
  35.2 0.0 copy-start
  35.2 2.0 %copy-done = bf16[3,3,3,256,256]{4,3,2,1,0:T(8,128)(2,1)S(1)} copy-done((bf16[3,3,3,256,256]{4,3,2,1,0:T(8,128)(2,1)S(1)}, bf16[3,3,3,256,256]{4,3,2,1,0:T(8,128)(2,1)}, u32[]{:S(2)}) %copy-start) | copy-done | bytes 3538968
  37.2 16.3 %cubes.1 = bf16[16,16,8,256]{3,2,1,0:T(8,128)(2,1)} custom-call(bf16[10,5,16,128]{3,2,1,0:T(8,128)(2,1)S(1)} %get-tuple-element.8.refs_0_, bf16[10,5,16,128]{3,2,1,0:T(8,128)(2,1)S(1)} %collective-permute-done.2.refs_1_, bf16[10,5,16,128]{3,2,1,0:T(8,128)(2,1)S(1)} %collective-permute-done.3.refs_2_, ...), custom_call_target="tpu_custom_call" | custom-call | tf_op jit(solution)/shard_map/cubes/pallas_call | solution.py:449
  (15 shorter events, 0.1 us)
Async XLA Ops:
  0.8 7.0 %collective-permute-start = (bf16[2,24,512]{2,1,0:T(8,128)(2,1)S(1)}, bf16[2,24,512]{2,1,0:T(8,128)(2,1)S(1)}, u32[]{:S(2)}, u32[]{:S(2)}) collective-permute-start(bf16[2,24,512]{2,1,0:T(8,128)(2,1)S(1)} %get-tuple-element.10), channel_id=1, source_target_pairs={{0,1},{2,3},{1,0},{3,2},{4,5},{6,7},{5,4},{7,6},{8,9},{10,11},{9,8... | collective-permute-start | bytes 147464 | tf_op jit(solution)/shard_map/ppermute | solution.py:394
  1.0 6.8 %collective-permute-start.1 = (bf16[2,24,512]{2,1,0:T(8,128)(2,1)S(1)}, bf16[2,24,512]{2,1,0:T(8,128)(2,1)S(1)}, u32[]{:S(2)}, u32[]{:S(2)}) collective-permute-start(bf16[2,24,512]{2,1,0:T(8,128)(2,1)S(1)} %get-tuple-element.9), channel_id=1, source_target_pairs={{1,2},{2,1},{5,6},{6,5},{9,10},{10,9},{13,14},{14,13},{17,18},{18,... | collective-permute-start | bytes 147464 | tf_op jit(solution)/shard_map/ppermute | solution.py:394
  5.4 2.5 %copy-start.3 = (bf16[2,128,512]{2,1,0:T(8,128)(2,1)S(1)}, bf16[2,128,512]{2,1,0:T(8,128)(2,1)}, u32[]{:S(2)}) copy-start(bf16[2,128,512]{2,1,0:T(8,128)(2,1)} %raw.1) | copy-start | bytes 786436
  7.9 1.4 %copy-start.2 = (bf16[2832,256]{1,0:T(8,128)(2,1)S(1)}, bf16[2832,256]{1,0:T(8,128)(2,1)}, u32[]{:S(2)}) copy-start(bf16[2832,256]{1,0:T(8,128)(2,1)} %weights.1.banded) | copy-start | bytes 4349956
  19.7 15.5 %copy-start.1 = (bf16[3,3,3,128,256]{4,3,2,1,0:T(8,128)(2,1)S(1)}, bf16[3,3,3,128,256]{4,3,2,1,0:T(8,128)(2,1)}, u32[]{:S(2)}) copy-start(bf16[3,3,3,128,256]{4,3,2,1,0:T(8,128)(2,1)} %refs_8_.1) | copy-start | bytes 5308420
  19.7 15.5 %copy-start.4 = (f32[256]{0:T(256)S(1)}, f32[256]{0:T(256)}, u32[]{:S(2)}) copy-start(f32[256]{0:T(256)} %param.19) | copy-start | bytes 3076
  19.8 15.4 %copy-start.5 = (f32[256]{0:T(256)S(1)}, f32[256]{0:T(256)}, u32[]{:S(2)}) copy-start(f32[256]{0:T(256)} %param.21) | copy-start | bytes 3076
  20.6 5.5 %collective-permute-start.2 = (bf16[10,5,16,128]{3,2,1,0:T(8,128)(2,1)}, bf16[10,5,16,128]{3,2,1,0:T(8,128)(2,1)S(1)}, u32[]{:S(2)}, u32[]{:S(2)}) collective-permute-start(bf16[10,5,16,128]{3,2,1,0:T(8,128)(2,1)} %get-tuple-element.7), channel_id=1, source_target_pairs={{0,8},{4,12},{8,0},{12,4},{16,24},{20,28},{24,16},{28,20},{1,9},{5... | collective-permute-start | bytes 614408 | tf_op jit(solution)/shard_map/ppermute | solution.py:439
  21.8 8.3 %collective-permute-start.3 = (bf16[10,5,16,128]{3,2,1,0:T(8,128)(2,1)S(1)}, bf16[10,5,16,128]{3,2,1,0:T(8,128)(2,1)S(1)}, u32[]{:S(2)}, u32[]{:S(2)}) collective-permute-start(bf16[10,5,16,128]{3,2,1,0:T(8,128)(2,1)S(1)} %get-tuple-element.6), channel_id=1, source_target_pairs={{0,16},{4,20},{8,24},{12,28},{16,0},{20,4},{24,8},{28,12},{1,17},{... | collective-permute-start | bytes 614408 | tf_op jit(solution)/shard_map/ppermute | solution.py:439
  22.0 11.7 %collective-permute-start.4 = (bf16[10,5,16,128]{3,2,1,0:T(8,128)(2,1)S(1)}, bf16[10,5,16,128]{3,2,1,0:T(8,128)(2,1)S(1)}, u32[]{:S(2)}, u32[]{:S(2)}) collective-permute-start(bf16[10,5,16,128]{3,2,1,0:T(8,128)(2,1)S(1)} %get-tuple-element.5), channel_id=1, source_target_pairs={{0,24},{4,28},{8,16},{12,20},{16,8},{20,12},{24,0},{28,4},{1,25},{... | collective-permute-start | bytes 614408 | tf_op jit(solution)/shard_map/ppermute | solution.py:439
  23.3 10.6 %collective-permute-start.5 = (bf16[6,5,16,128]{3,2,1,0:T(8,128)(2,1)S(1)}, bf16[6,5,16,128]{3,2,1,0:T(8,128)(2,1)S(1)}, u32[]{:S(2)}, u32[]{:S(2)}) collective-permute-start(bf16[6,5,16,128]{3,2,1,0:T(8,128)(2,1)S(1)} %dynamic-slice_bitcast_fusion.4), channel_id=1, source_target_pairs={{0,4},{4,0},{8,12},{12,8},{16,20},{20,16},{24,28},{28,24},{1,5},{5... | collective-permute-start | bytes 368648 | tf_op jit(solution)/shard_map/ppermute | solution.py:442
  26.1 7.7 %collective-permute-start.6 = (bf16[6,5,16,128]{3,2,1,0:T(8,128)(2,1)S(1)}, bf16[6,5,16,128]{3,2,1,0:T(8,128)(2,1)S(1)}, u32[]{:S(2)}, u32[]{:S(2)}) collective-permute-start(bf16[6,5,16,128]{3,2,1,0:T(8,128)(2,1)S(1)} %constant_dynamic-slice_fusion.2), channel_id=1, source_target_pairs={{0,4},{4,0},{8,12},{12,8},{16,20},{20,16},{24,28},{28,24},{1,5},{5... | collective-permute-start | bytes 368648 | tf_op jit(solution)/shard_map/ppermute | solution.py:442
  30.2 4.6 %collective-permute-start.7 = (bf16[6,5,16,128]{3,2,1,0:T(8,128)(2,1)S(1)}, bf16[6,5,16,128]{3,2,1,0:T(8,128)(2,1)S(1)}, u32[]{:S(2)}, u32[]{:S(2)}) collective-permute-start(bf16[6,5,16,128]{3,2,1,0:T(8,128)(2,1)S(1)} %constant_dynamic-slice_fusion.1), channel_id=1, source_target_pairs={{0,4},{4,0},{8,12},{12,8},{16,20},{20,16},{24,28},{28,24},{1,5},{5... | collective-permute-start | bytes 368648 | tf_op jit(solution)/shard_map/ppermute | solution.py:442
  33.8 1.4 %collective-permute-start.8 = (bf16[6,5,16,128]{3,2,1,0:T(8,128)(2,1)S(1)}, bf16[6,5,16,128]{3,2,1,0:T(8,128)(2,1)S(1)}, u32[]{:S(2)}, u32[]{:S(2)}) collective-permute-start(bf16[6,5,16,128]{3,2,1,0:T(8,128)(2,1)S(1)} %constant_dynamic-slice_fusion), channel_id=1, source_target_pairs={{0,4},{4,0},{8,12},{12,8},{16,20},{20,16},{24,28},{28,24},{1,5},{5... | collective-permute-start | bytes 368648 | tf_op jit(solution)/shard_map/ppermute | solution.py:442
  35.2 2.0 %copy-start = (bf16[3,3,3,256,256]{4,3,2,1,0:T(8,128)(2,1)S(1)}, bf16[3,3,3,256,256]{4,3,2,1,0:T(8,128)(2,1)}, u32[]{:S(2)}) copy-start(bf16[3,3,3,256,256]{4,3,2,1,0:T(8,128)(2,1)} %refs_10_.1) | copy-start | bytes 10616836

commit v2 on v1

--- a/solution.py
+++ b/solution.py
@@ -256,10 +256,32 @@
                         out[d, at, i] = part[w]
 
 
+def filter_kernel(send, w, u, window):
+    me = lax.axis_index("gz")
+    pairs = window.shape[0]
+    window[...] = send[me // 2, pl.ds((1 - me % 2) * (pairs - 2), pairs)]
+    chan = w.shape[3]
+    for kx in range(3):
+        for dz in range(3):
+            at = slice((3 * kx + dz) * chan, (3 * kx + dz + 1) * chan)
+            g0, g1, g2 = (w[dz, ky, kx].astype(F32) for ky in range(3))
+            outer, inner = 0.5 * (g0 + g2), 0.5 * g1
+            u[0, at] = w[dz, 0, kx]
+            u[1, at] = (outer + inner).astype(BF16)
+            u[2, at] = (outer - inner).astype(BF16)
+            u[3, at] = w[dz, 2, kx]
+
+
+def four_rows(x):
+    x = x.reshape((x.shape[0] // 2, 2) + x.shape[1:])
+    even, odd = x[:, 0], x[:, 1]
+    return (even[:-1] - even[1:], odd[:-1] + even[1:], even[1:] - odd[:-1], odd[:-1] - odd[1:])
+
+
 def cube_kernel(cfg, *refs):
     sources, zl, third_rows, vb, in_chan, mid_chan, out_chan, flip = cfg
     near, far = refs[: sources // 2], refs[sources // 2 : sources]
-    wa, ba, wb, bb, out, a3, b3 = refs[sources:]
+    wa, ba, ub, bb, out, a3, mid, vm, ms = refs[sources:]
     me = lax.axis_index("gz")
     depth = sources * zl
     xs = 2 * vb
@@ -294,78 +316,79 @@
     taps = [(ky, kx) for ky in range(3) for kx in range(3)]
     mid_x = xs + 2
     mid_rows = third_rows + 2
-    step_rows = 9 if mid_rows % 9 == 0 else 1
+    step = 9 if mid_rows % 9 == 0 else 1
 
     def iso_a(c, _):
-        y0 = c * step_rows
-        n = step_rows * mid_x * depth
-        x = jnp.concatenate(
-            [a3[pl.ds(y0 + ky, step_rows), kx : kx + mid_x].reshape(n, 3 * in_chan) for ky, kx in taps], axis=1
-        )
+        first = c * step
+        n = step * mid_x * depth
+        x = jnp.concatenate([a3[pl.ds(first + ky, step), kx : kx + mid_x].reshape(n, 3 * in_chan) for ky, kx in taps], axis=1)
         w = jnp.concatenate([wa[dz, ky, kx] for ky, kx in taps for dz in range(3)], axis=0)
-        y = jnp.dot(x, w, preferred_element_type=F32)
-        y = jnp.maximum(y + ba[...], 0.0)
-        here = (step_rows, mid_x, depth, mid_chan)
-        b3[pl.ds(y0, step_rows), :, :, mid_chan : 2 * mid_chan] = y.reshape(here).astype(BF16)
-        y = y.reshape(step_rows * mid_x, depth // 8, 8, mid_chan)
-        sub = lax.broadcasted_iota(jnp.int32, y.shape, 2)
-        none = jnp.zeros_like(y[:, :1])
-        rolled = pltpu.roll(y, 1, 2)
-        other = jnp.concatenate([none, rolled[:, :-1]], axis=1)
-        down = jnp.where(sub == 0, other, rolled)
-        b3[pl.ds(y0, step_rows), :, :, 0:mid_chan] = down.reshape(here).astype(BF16)
-        rolled = pltpu.roll(y, 7, 2)
-        other = jnp.concatenate([rolled[:, 1:], none], axis=1)
-        up = jnp.where(sub == 7, other, rolled)
-        b3[pl.ds(y0, step_rows), :, :, 2 * mid_chan : 3 * mid_chan] = up.reshape(here).astype(BF16)
+        y = jnp.maximum(jnp.dot(x, w, preferred_element_type=F32) + ba[...], 0.0)
+        mid[pl.ds(first, step)] = y.reshape(step, mid_x, depth, mid_chan).astype(BF16)
         return 0
 
-    lax.fori_loop(0, mid_rows // step_rows, iso_a, 0)
+    lax.fori_loop(0, mid_rows // step, iso_a, 0)
+
+    def products(v, u, first, count, breadth, chan):
+        n = count * breadth * depth
+        slot = (first // count) % 2
+        for t in range(4):
+            x = jnp.concatenate([v[t, first : first + count, kx : kx + breadth].reshape(n, 3 * chan) for kx in range(3)], axis=1)
+            ms[slot, t, 0:n] = jnp.dot(x, u[t], preferred_element_type=F32)
+        m1, m2 = ms[slot, 1, 0:n], ms[slot, 2, 0:n]
+        return ms[slot, 0, 0:n] + (m1 + m2), (m1 - m2) - ms[slot, 3, 0:n]
 
     row, col = lax.axis_index("xy"), lax.axis_index("gz")
 
     @pl.when(row == 0)
     def _():
-        b3[0] = jnp.zeros(b3.shape[1:], BF16)
+        mid[0] = jnp.zeros(mid.shape[1:], BF16)
 
     @pl.when(row == lax.axis_size("xy") - 1)
     def _():
-        b3[mid_rows - 1] = jnp.zeros(b3.shape[1:], BF16)
+        mid[mid_rows - 1] = jnp.zeros(mid.shape[1:], BF16)
 
     @pl.when(col == 0)
     def _():
-        b3[:, 0] = jnp.zeros((mid_rows,) + b3.shape[2:], BF16)
+        mid[:, 0] = jnp.zeros(mid.shape[:1] + mid.shape[2:], BF16)
 
     @pl.when(col == lax.axis_size("gz") - 1)
     def _():
-        b3[:, mid_x - 1] = jnp.zeros((mid_rows,) + b3.shape[2:], BF16)
-
+        mid[:, mid_x - 1] = jnp.zeros(mid.shape[:1] + mid.shape[2:], BF16)
+
+    pairs_b = third_rows // 2
+    step = 4 if pairs_b % 4 == 0 else 1
     if flip:
         n = xs * depth
         to = lax.broadcasted_iota(jnp.int32, (n, n), 0)
         at = lax.broadcasted_iota(jnp.int32, (n, n), 1)
         turn = jnp.where((to // xs == at % depth) & (to % xs == at // depth), 1.0, 0.0).astype(BF16)
-    out_rows = 8
-
-    def iso_b(c, _):
-        y0 = c * out_rows
-        n = out_rows * xs * depth
-        x = jnp.concatenate(
-            [b3[pl.ds(y0 + ky, out_rows), kx : kx + xs].reshape(n, 3 * mid_chan) for ky, kx in taps], axis=1
-        )
-        w = jnp.concatenate([wb[dz, ky, kx] for ky, kx in taps for dz in range(3)], axis=0)
-        y = jnp.dot(x, w, preferred_element_type=F32)
-        y = jnp.maximum(y + bb[...], 0.0).astype(BF16)
-        if flip:
-            y = y.reshape(out_rows, xs * depth, out_chan)
-            for i in range(out_rows):
-                t = jnp.dot(turn, y[i], preferred_element_type=F32).astype(BF16)
-                out[:, y0 + i] = t.reshape(depth, xs, out_chan)
-        else:
-            out[pl.ds(y0, out_rows)] = y.reshape(out_rows, xs, depth, out_chan)
-        return 0
-
-    lax.fori_loop(0, third_rows // out_rows, iso_b, 0)
+    for first in range(0, pairs_b, step):
+        for x_at in range(mid_x):
+            x = mid[2 * first : 2 * (first + step) + 2, x_at].astype(F32)
+            for t, v in enumerate(four_rows(x)):
+                here = v.shape
+                vm[t, first : first + step, x_at, :, mid_chan : 2 * mid_chan] = v.astype(BF16)
+                v = v.reshape(step, depth // 8, 8, mid_chan)
+                sub = lax.broadcasted_iota(jnp.int32, v.shape, 2)
+                none = jnp.zeros_like(v[:, :1])
+                rolled = pltpu.roll(v, 1, 2)
+                moved = jnp.where(sub == 0, jnp.concatenate([none, rolled[:, :-1]], axis=1), rolled)
+                vm[t, first : first + step, x_at, :, 0:mid_chan] = moved.reshape(here).astype(BF16)
+                rolled = pltpu.roll(v, 7, 2)
+                moved = jnp.where(sub == 7, jnp.concatenate([rolled[:, 1:], none], axis=1), rolled)
+                vm[t, first : first + step, x_at, :, 2 * mid_chan :] = moved.reshape(here).astype(BF16)
+        for i, y in enumerate(products(vm, ub, first, step, xs, mid_chan)):
+            y = jnp.maximum(y + bb[...], 0.0).astype(BF16)
+            if flip:
+                y = y.reshape(step, xs * depth, out_chan)
+                for j in range(step):
+                    t = jnp.dot(turn, y[j], preferred_element_type=F32).astype(BF16)
+                    out[:, 2 * (first + j) + i] = t.reshape(depth, xs, out_chan)
+            else:
+                y = y.reshape(step, xs, depth, out_chan)
+                for j in range(step):
+                    out[2 * (first + j) + i] = y[j]
 
 
 def body(
@@ -432,13 +455,25 @@
     )(first, raw_volume, second, banded)
     me = lax.axis_index("gz")
     other = (1 - me % 2) * vb
+    ub, own = pl.pallas_call(
+        filter_kernel,
+        out_shape=[
+            jax.ShapeDtypeStruct((4, 9 * weight_iso_b.shape[3], weight_iso_b.shape[4]), BF16),
+            jax.ShapeDtypeStruct((vb + 2,) + send.shape[2:], BF16),
+        ],
+        in_specs=[VMEM, VMEM],
+        out_specs=[VMEM, VMEM],
+        compiler_params=pltpu.CompilerParams(vmem_limit_bytes=20 << 20),
+        cost_estimate=pl.CostEstimate(flops=4000000000, bytes_accessed=8000000, transcendentals=0),
+        name="filters",
+    )(send, weight_iso_b)
     near, far = [], []
     for k in range(chips):
         block = lax.dynamic_index_in_dim(send, (me // 2) ^ k, 0, keepdims=False)
         if k:
             block = lax.ppermute(block, "gz", [(i, i ^ (2 * k)) for i in range(dests)])
         near.append(block)
-        window = lax.dynamic_slice_in_dim(block, other, vb + 2, axis=0)
+        window = lax.dynamic_slice_in_dim(block, other, vb + 2, axis=0) if k else own
         far.append(lax.ppermute(window, "gz", [(i, i ^ 1) for i in range(dests)]))
 
     xs = 2 * vb
@@ -453,11 +488,13 @@
         out_specs=VMEM,
         scratch_shapes=[
             pltpu.VMEM((third_rows + 4, xs + 4, depth, 3 * in_chan), BF16),
-            pltpu.VMEM((third_rows + 2, xs + 2, depth, 3 * mid_chan), BF16),
+            pltpu.VMEM((third_rows + 2, xs + 2, depth, mid_chan), BF16),
+            pltpu.VMEM((4, third_rows // 2, xs + 2, depth, 3 * mid_chan), BF16),
+            pltpu.VMEM((2, 4, 4 * xs * depth, mid_chan), F32),
         ],
-        compiler_params=pltpu.CompilerParams(vmem_limit_bytes=(20 if depth <= 16 else 48) << 20),
+        compiler_params=pltpu.CompilerParams(vmem_limit_bytes=(36 if depth <= 16 else 60) << 20),
         name="cubes",
-    )(*near, *far, weight_iso_a, bias_iso_a[None], weight_iso_b, bias_iso_b[None])
+    )(*near, *far, weight_iso_a, bias_iso_a[None], ub, bias_iso_b[None])
     return out if flip else jnp.transpose(out, (2, 0, 1, 3))
 
 

time: 53.8 us -> 48.8 us (0.907)
  the two profiles are of different devices: /device:TPU:13 before, /device:TPU:0 now
where the time goes in v2:
time: 48.8 us; the launch traced here: 48.6 us
  Pallas kernels  27.2 us (56%)
  starting transfers between devices  10.9 us (22%)
  waiting for transfers between devices  8.05 us (16%)
  local copies, waits for them, and re-layouts  2.39 us (5%)
    pallas_call x1, Pallas kernels, body(): pl.pallas_call(functools.partial(cube_kernel, (dests, zl, third_rows, vb,...  13.4 us
    pallas_call x1, Pallas kernels, body(): pl.pallas_call(functools.partial(plane_kernel, (zl, rows, width, chips, 2...  10.5 us
    ppermute x3, waiting for transfers between devices, body(): block = lax.ppermute(block, 'gz', [(i, i ^ 2 * k) for i in range(dests)])  7.07 us
    ppermute x2, starting transfers between devices, swap(): lax.ppermute(edge, 'xy', [(i, i + 1) for i in pairs] + [(i + 1, i) for i...  6.56 us
    ppermute x3, starting transfers between devices, body(): block = lax.ppermute(block, 'gz', [(i, i ^ 2 * k) for i in range(dests)])  3.55 us
    pallas_call x1, Pallas kernels, body(): pl.pallas_call(weight_kernel, out_shape=jax.ShapeDtypeStruct((BIAS + 16,...  2.46 us
    unnamed x12, local copies, waits for them, and re-layouts  1.38 us
  transfers between devices with their start and end apart: 9, of which 4 were waited for; matrix products, arithmetic and copies ran while one was open for 0% of the time, Pallas kernels for 7%

profile of v2, /device:TPU:0, one launch (start us, length us, event | category | flops | bytes accessed | tf_op | source)
XLA Modules:
  0.0 48.6 jit_solution(15139615019851131904)
XLA Ops:
  0.0 0.8 %constant_dynamic-slice_fusion.3 = (bf16[2,24,512]{2,1,0:T(8,128)(2,1)S(1)}, bf16[2,24,512]{2,1,0:T(8,128)(2,1)S(1)}) fusion(bf16[2,128,512]{2,1,0:T(8,128)(2,1)} %raw.1, s32[]{:T(128)S(6)} %select_n.47, s32[]{:T(128)S(6)} %select_n.46), kind=kLoop, calls=%fused_computation.7 | loop fusion | bytes 196616 | tf_op jit(solution)/shard_map/dynamic_slice | solution.py:416
  0.8 0.7 %collective-permute-start.1 = (bf16[2,24,512]{2,1,0:T(8,128)(2,1)S(1)}, bf16[2,24,512]{2,1,0:T(8,128)(2,1)S(1)}, u32[]{:S(2)}, u32[]{:S(2)}) collective-permute-start(bf16[2,24,512]{2,1,0:T(8,128)(2,1)S(1)} %get-tuple-element.13), channel_id=1, source_target_pairs={{1,2},{2,1},{5,6},{6,5},{9,10},{10,9},{13,14},{14,13},{17,18},{18,... | collective-permute-start | bytes 147464 | tf_op jit(solution)/shard_map/ppermute | solution.py:417
  1.5 5.9 %collective-permute-start = (bf16[2,24,512]{2,1,0:T(8,128)(2,1)S(1)}, bf16[2,24,512]{2,1,0:T(8,128)(2,1)S(1)}, u32[]{:S(2)}, u32[]{:S(2)}) collective-permute-start(bf16[2,24,512]{2,1,0:T(8,128)(2,1)S(1)} %get-tuple-element.14), channel_id=1, source_target_pairs={{0,1},{2,3},{1,0},{3,2},{4,5},{6,7},{5,4},{7,6},{8,9},{10,11},{9,8... | collective-permute-start | bytes 147464 | tf_op jit(solution)/shard_map/ppermute | solution.py:417
  7.4 2.5 %weights.1.banded = bf16[2832,256]{1,0:T(8,128)(2,1)} custom-call(bf16[3,3,32]{2,1,0:T(4,128)(2,1)} %bitcast.22, f32[1,32]{1,0:T(1,128)} %bitcast.23, bf16[3,3,32,64]{3,2,1,0:T(8,128)(2,1)} %bitcast.21, f32[1,64]{1,0:T(1,128)} %bitcast.24, bf16[3,3,64,128]{3,2,1,0:T(8,128)(2,1)} %bitcast.20, f32[1,128]{1,0:T(1,128)} %bitcast.25), custom_call_target="tpu_custom_call" | custom-call | flops 2000000000 | bytes 2000000 | tf_op jit(solution)/shard_map/weights/pallas_call | solution.py:426
  9.9 0.0 collective-permute-done.swap_a
  9.9 1.4 %copy-done.1 = bf16[2832,256]{1,0:T(8,128)(2,1)S(1)} copy-done((bf16[2832,256]{1,0:T(8,128)(2,1)S(1)}, bf16[2832,256]{1,0:T(8,128)(2,1)}, u32[]{:S(2)}) %copy-start.1) | copy-done | bytes 1450008
  11.2 10.5 %planes.1.send = bf16[4,10,5,16,128]{4,3,2,1,0:T(8,128)(2,1)S(1)} custom-call(bf16[2,24,512]{2,1,0:T(8,128)(2,1)S(1)} %collective-permute-done.swap_a, bf16[2,128,512]{2,1,0:T(8,128)(2,1)S(1)} %copy-done.2, bf16[2,24,512]{2,1,0:T(8,128)(2,1)S(1)} %collective-permute-done.1.swap_b, bf16[2832,256]{1,0:T(8,128)(2,1)S(1)} %copy-done.1), custom_call_target="tpu_custom_call" | custom-call | tf_op jit(solution)/shard_map/planes/pallas_call | solution.py:441
  21.8 0.2 dynamic-slice_bitcast_fusion
  21.9 2.5 %collective-permute-start.4 = (bf16[10,5,16,128]{3,2,1,0:T(8,128)(2,1)S(1)}, bf16[10,5,16,128]{3,2,1,0:T(8,128)(2,1)S(1)}, u32[]{:S(2)}, u32[]{:S(2)}) collective-permute-start(bf16[10,5,16,128]{3,2,1,0:T(8,128)(2,1)S(1)} %get-tuple-element.9), channel_id=1, source_target_pairs={{0,24},{4,28},{8,16},{12,20},{16,8},{20,12},{24,0},{28,4},{1,25},{... | collective-permute-start | bytes 614408 | tf_op jit(solution)/shard_map/ppermute | solution.py:474
  24.4 0.5 %collective-permute-start.3 = (bf16[10,5,16,128]{3,2,1,0:T(8,128)(2,1)S(1)}, bf16[10,5,16,128]{3,2,1,0:T(8,128)(2,1)S(1)}, u32[]{:S(2)}, u32[]{:S(2)}) collective-permute-start(bf16[10,5,16,128]{3,2,1,0:T(8,128)(2,1)S(1)} %get-tuple-element.10), channel_id=1, source_target_pairs={{0,16},{4,20},{8,24},{12,28},{16,0},{20,4},{24,8},{28,12},{1,17},{... | collective-permute-start | bytes 614408 | tf_op jit(solution)/shard_map/ppermute | solution.py:474
  24.9 0.5 %collective-permute-start.2 = (bf16[10,5,16,128]{3,2,1,0:T(8,128)(2,1)S(1)}, bf16[10,5,16,128]{3,2,1,0:T(8,128)(2,1)S(1)}, u32[]{:S(2)}, u32[]{:S(2)}) collective-permute-start(bf16[10,5,16,128]{3,2,1,0:T(8,128)(2,1)S(1)} %get-tuple-element.11), channel_id=1, source_target_pairs={{0,8},{4,12},{8,0},{12,4},{16,24},{20,28},{24,16},{28,20},{1,9},{5... | collective-permute-start | bytes 614408 | tf_op jit(solution)/shard_map/ppermute | solution.py:474
  25.5 0.8 %filters.1 = (bf16[4,2304,256]{2,1,0:T(8,128)(2,1)S(1)}, bf16[6,5,16,128]{3,2,1,0:T(8,128)(2,1)S(1)}) custom-call(bf16[4,10,5,16,128]{4,3,2,1,0:T(8,128)(2,1)S(1)} %planes.1.send, bf16[3,3,3,256,256]{4,3,2,1,0:T(8,128)(2,1)S(1)} %copy-done.5), custom_call_target="tpu_custom_call" | custom-call | flops 4000000000 | bytes 8000000 | tf_op jit(solution)/shard_map/filters/pallas_call | solution.py:458
  26.3 0.1 collective-permute-start.5
  26.4 4.5 %collective-permute-done.4.refs_3_ = bf16[10,5,16,128]{3,2,1,0:T(8,128)(2,1)S(1)} collective-permute-done((bf16[10,5,16,128]{3,2,1,0:T(8,128)(2,1)S(1)}, bf16[10,5,16,128]{3,2,1,0:T(8,128)(2,1)S(1)}, u32[]{:S(2)}, u32[]{:S(2)}) %collective-permute-start.4) | collective-permute-done | bytes 204832 | tf_op jit(solution)/shard_map/ppermute | solution.py:474
  30.9 0.1 collective-permute-start.8
  31.0 2.5 %collective-permute-done.3.refs_2_ = bf16[10,5,16,128]{3,2,1,0:T(8,128)(2,1)S(1)} collective-permute-done((bf16[10,5,16,128]{3,2,1,0:T(8,128)(2,1)S(1)}, bf16[10,5,16,128]{3,2,1,0:T(8,128)(2,1)S(1)}, u32[]{:S(2)}, u32[]{:S(2)}) %collective-permute-start.3) | collective-permute-done | bytes 204832 | tf_op jit(solution)/shard_map/ppermute | solution.py:474
  33.5 0.1 collective-permute-start.7
  33.6 0.0 collective-permute-done.2.refs_1_
  33.7 0.5 %collective-permute-start.6 = (bf16[6,5,16,128]{3,2,1,0:T(8,128)(2,1)S(1)}, bf16[6,5,16,128]{3,2,1,0:T(8,128)(2,1)S(1)}, u32[]{:S(2)}, u32[]{:S(2)}) collective-permute-start(bf16[6,5,16,128]{3,2,1,0:T(8,128)(2,1)S(1)} %constant_dynamic-slice_fusion.2), channel_id=1, source_target_pairs={{0,4},{4,0},{8,12},{12,8},{16,20},{20,16},{24,28},{28,24},{1,5},{5... | collective-permute-start | bytes 368648 | tf_op jit(solution)/shard_map/ppermute | solution.py:477
  34.2 0.0 collective-permute-done.5.refs_4_
  34.2 0.0 collective-permute-done.8.refs_7_
  34.2 0.7 %collective-permute-done.7.refs_6_ = bf16[6,5,16,128]{3,2,1,0:T(8,128)(2,1)S(1)} collective-permute-done((bf16[6,5,16,128]{3,2,1,0:T(8,128)(2,1)S(1)}, bf16[6,5,16,128]{3,2,1,0:T(8,128)(2,1)S(1)}, u32[]{:S(2)}, u32[]{:S(2)}) %collective-permute-start.7) | collective-permute-done | bytes 122912 | tf_op jit(solution)/shard_map/ppermute | solution.py:477
  34.9 0.2 collective-permute-done.6.refs_5_
  35.2 13.4 %cubes.1 = bf16[16,16,8,256]{3,2,1,0:T(8,128)(2,1)} custom-call(bf16[10,5,16,128]{3,2,1,0:T(8,128)(2,1)S(1)} %get-tuple-element.12.refs_0_, bf16[10,5,16,128]{3,2,1,0:T(8,128)(2,1)S(1)} %collective-permute-done.2.refs_1_, bf16[10,5,16,128]{3,2,1,0:T(8,128)(2,1)S(1)} %collective-permute-done.3.refs_2_, ...), custom_call_target="tpu_custom_call" | custom-call | tf_op jit(solution)/shard_map/cubes/pallas_call | solution.py:484
  (15 shorter events, 0.0 us)
Async XLA Ops:
  0.8 9.0 %collective-permute-start.1 = (bf16[2,24,512]{2,1,0:T(8,128)(2,1)S(1)}, bf16[2,24,512]{2,1,0:T(8,128)(2,1)S(1)}, u32[]{:S(2)}, u32[]{:S(2)}) collective-permute-start(bf16[2,24,512]{2,1,0:T(8,128)(2,1)S(1)} %get-tuple-element.13), channel_id=1, source_target_pairs={{1,2},{2,1},{5,6},{6,5},{9,10},{10,9},{13,14},{14,13},{17,18},{18,... | collective-permute-start | bytes 147464 | tf_op jit(solution)/shard_map/ppermute | solution.py:417
  1.5 8.4 %collective-permute-start = (bf16[2,24,512]{2,1,0:T(8,128)(2,1)S(1)}, bf16[2,24,512]{2,1,0:T(8,128)(2,1)S(1)}, u32[]{:S(2)}, u32[]{:S(2)}) collective-permute-start(bf16[2,24,512]{2,1,0:T(8,128)(2,1)S(1)} %get-tuple-element.14), channel_id=1, source_target_pairs={{0,1},{2,3},{1,0},{3,2},{4,5},{6,7},{5,4},{7,6},{8,9},{10,11},{9,8... | collective-permute-start | bytes 147464 | tf_op jit(solution)/shard_map/ppermute | solution.py:417
  7.4 2.5 %copy-start.2 = (bf16[2,128,512]{2,1,0:T(8,128)(2,1)S(1)}, bf16[2,128,512]{2,1,0:T(8,128)(2,1)}, u32[]{:S(2)}) copy-start(bf16[2,128,512]{2,1,0:T(8,128)(2,1)} %raw.1) | copy-start | bytes 786436
  9.9 1.4 %copy-start.1 = (bf16[2832,256]{1,0:T(8,128)(2,1)S(1)}, bf16[2832,256]{1,0:T(8,128)(2,1)}, u32[]{:S(2)}) copy-start(bf16[2832,256]{1,0:T(8,128)(2,1)} %weights.1.banded) | copy-start | bytes 4349956
  11.2 14.2 %copy-start.5 = (bf16[3,3,3,256,256]{4,3,2,1,0:T(8,128)(2,1)S(1)}, bf16[3,3,3,256,256]{4,3,2,1,0:T(8,128)(2,1)}, u32[]{:S(2)}) copy-start(bf16[3,3,3,256,256]{4,3,2,1,0:T(8,128)(2,1)} %w.1) | copy-start | bytes 10616836
  21.9 9.0 %collective-permute-start.4 = (bf16[10,5,16,128]{3,2,1,0:T(8,128)(2,1)S(1)}, bf16[10,5,16,128]{3,2,1,0:T(8,128)(2,1)S(1)}, u32[]{:S(2)}, u32[]{:S(2)}) collective-permute-start(bf16[10,5,16,128]{3,2,1,0:T(8,128)(2,1)S(1)} %get-tuple-element.9), channel_id=1, source_target_pairs={{0,24},{4,28},{8,16},{12,20},{16,8},{20,12},{24,0},{28,4},{1,25},{... | collective-permute-start | bytes 614408 | tf_op jit(solution)/shard_map/ppermute | solution.py:474
  24.4 9.1 %collective-permute-start.3 = (bf16[10,5,16,128]{3,2,1,0:T(8,128)(2,1)S(1)}, bf16[10,5,16,128]{3,2,1,0:T(8,128)(2,1)S(1)}, u32[]{:S(2)}, u32[]{:S(2)}) collective-permute-start(bf16[10,5,16,128]{3,2,1,0:T(8,128)(2,1)S(1)} %get-tuple-element.10), channel_id=1, source_target_pairs={{0,16},{4,20},{8,24},{12,28},{16,0},{20,4},{24,8},{28,12},{1,17},{... | collective-permute-start | bytes 614408 | tf_op jit(solution)/shard_map/ppermute | solution.py:474
  24.9 10.2 %copy-start = (bf16[3,3,3,128,256]{4,3,2,1,0:T(8,128)(2,1)S(1)}, bf16[3,3,3,128,256]{4,3,2,1,0:T(8,128)(2,1)}, u32[]{:S(2)}) copy-start(bf16[3,3,3,128,256]{4,3,2,1,0:T(8,128)(2,1)} %refs_8_.1) | copy-start | bytes 5308420
  24.9 10.2 %copy-start.3 = (f32[256]{0:T(256)S(1)}, f32[256]{0:T(256)}, u32[]{:S(2)}) copy-start(f32[256]{0:T(256)} %param.19) | copy-start | bytes 3076
  24.9 10.2 %copy-start.4 = (f32[256]{0:T(256)S(1)}, f32[256]{0:T(256)}, u32[]{:S(2)}) copy-start(f32[256]{0:T(256)} %param.21) | copy-start | bytes 3076
  24.9 8.7 %collective-permute-start.2 = (bf16[10,5,16,128]{3,2,1,0:T(8,128)(2,1)S(1)}, bf16[10,5,16,128]{3,2,1,0:T(8,128)(2,1)S(1)}, u32[]{:S(2)}, u32[]{:S(2)}) collective-permute-start(bf16[10,5,16,128]{3,2,1,0:T(8,128)(2,1)S(1)} %get-tuple-element.11), channel_id=1, source_target_pairs={{0,8},{4,12},{8,0},{12,4},{16,24},{20,28},{24,16},{28,20},{1,9},{5... | collective-permute-start | bytes 614408 | tf_op jit(solution)/shard_map/ppermute | solution.py:474
  26.3 7.9 %collective-permute-start.5 = (bf16[6,5,16,128]{3,2,1,0:T(8,128)(2,1)S(1)}, bf16[6,5,16,128]{3,2,1,0:T(8,128)(2,1)S(1)}, u32[]{:S(2)}, u32[]{:S(2)}) collective-permute-start(bf16[6,5,16,128]{3,2,1,0:T(8,128)(2,1)S(1)} %get-tuple-element.7), channel_id=1, source_target_pairs={{0,4},{4,0},{8,12},{12,8},{16,20},{20,16},{24,28},{28,24},{1,5},{5... | collective-permute-start | bytes 368648 | tf_op jit(solution)/shard_map/ppermute | solution.py:477
  30.9 3.3 %collective-permute-start.8 = (bf16[6,5,16,128]{3,2,1,0:T(8,128)(2,1)S(1)}, bf16[6,5,16,128]{3,2,1,0:T(8,128)(2,1)S(1)}, u32[]{:S(2)}, u32[]{:S(2)}) collective-permute-start(bf16[6,5,16,128]{3,2,1,0:T(8,128)(2,1)S(1)} %constant_dynamic-slice_fusion), channel_id=1, source_target_pairs={{0,4},{4,0},{8,12},{12,8},{16,20},{20,16},{24,28},{28,24},{1,5},{5... | collective-permute-start | bytes 368648 | tf_op jit(solution)/shard_map/ppermute | solution.py:477
  33.5 1.4 %collective-permute-start.7 = (bf16[6,5,16,128]{3,2,1,0:T(8,128)(2,1)S(1)}, bf16[6,5,16,128]{3,2,1,0:T(8,128)(2,1)S(1)}, u32[]{:S(2)}, u32[]{:S(2)}) collective-permute-start(bf16[6,5,16,128]{3,2,1,0:T(8,128)(2,1)S(1)} %constant_dynamic-slice_fusion.1), channel_id=1, source_target_pairs={{0,4},{4,0},{8,12},{12,8},{16,20},{20,16},{24,28},{28,24},{1,5},{5... | collective-permute-start | bytes 368648 | tf_op jit(solution)/shard_map/ppermute | solution.py:477
  33.7 1.5 %collective-permute-start.6 = (bf16[6,5,16,128]{3,2,1,0:T(8,128)(2,1)S(1)}, bf16[6,5,16,128]{3,2,1,0:T(8,128)(2,1)S(1)}, u32[]{:S(2)}, u32[]{:S(2)}) collective-permute-start(bf16[6,5,16,128]{3,2,1,0:T(8,128)(2,1)S(1)} %constant_dynamic-slice_fusion.2), channel_id=1, source_target_pairs={{0,4},{4,0},{8,12},{12,8},{16,20},{20,16},{24,28},{28,24},{1,5},{5... | collective-permute-start | bytes 368648 | tf_op jit(solution)/shard_map/ppermute | solution.py:477

commit v3 on v2

--- a/solution.py
+++ b/solution.py
@@ -39,12 +39,9 @@
     return x + pltpu.roll(x, 32, 1) + pltpu.roll(x, 64, 1) + pltpu.roll(x, 96, 1)
 
 
-def weight_kernel(w1, b1, w2, b2, w3, b3, banded, small):
-    small[...] = jnp.zeros_like(small)
-    for ky in range(3):
-        small[3 * ky : 3 * ky + 3, 0:32] = w1[ky].astype(F32)
-    small[9:10, 0:32] = b1[...]
-    small[10:11, 0:64] = b2[...]
+def weight_kernel(packed, biases, banded, small):
+    small[0:16] = packed[864:880].astype(F32)
+    small[9:11] = biases[0:2]
     tap = []
     for i in range(10):
         x = tile_lanes(small, i)
@@ -53,7 +50,7 @@
     x = small[10:11, :]
     x = x + pltpu.roll(x, 64, 1)
     row = lax.broadcasted_iota(jnp.int32, (16, 256), 0)
-    rest = jnp.where(row < 3, tap[9], jnp.where(row < 6, jnp.concatenate([x, x], axis=1), jnp.concatenate([b3[...]] * 2, axis=1)))
+    rest = jnp.where(row < 3, tap[9], jnp.where(row < 6, jnp.concatenate([x, x], axis=1), jnp.concatenate([biases[2:3]] * 2, axis=1)))
     high = rest.astype(BF16).astype(F32)
     mid = (rest - high).astype(BF16).astype(F32)
     low = rest - high - mid
@@ -72,7 +69,8 @@
 
     for ky in range(3):
         for kx in range(3):
-            w = w2[ky, kx]
+            at = 576 + 32 * (3 * ky + kx)
+            w = packed[at : at + 32, 0:64]
             for dy in range(2):
                 for dx in range(2):
                     r, c = ky + dy, kx + dx
@@ -81,7 +79,8 @@
                     banded[at : at + 32, lanes] = w
                     at = T2 + 512 + 128 * r + 32 * ((c + 2) % 4)
                     banded[at : at + 32, lanes] = w
-            w = w3[ky, kx]
+            at = 64 * (3 * ky + kx)
+            w = packed[at : at + 64, :]
             for dx in range(2):
                 at = T3 + 256 * ky + 64 * (kx + dx)
                 banded[at : at + 64, 128 * dx : 128 * dx + 128] = w
@@ -256,32 +255,42 @@
                         out[d, at, i] = part[w]
 
 
-def filter_kernel(send, w, u, window):
+def filter_kernel(send, wa, wb, ua, ub, sums, window):
     me = lax.axis_index("gz")
     pairs = window.shape[0]
     window[...] = send[me // 2, pl.ds((1 - me % 2) * (pairs - 2), pairs)]
-    chan = w.shape[3]
-    for kx in range(3):
-        for dz in range(3):
-            at = slice((3 * kx + dz) * chan, (3 * kx + dz + 1) * chan)
-            g0, g1, g2 = (w[dz, ky, kx].astype(F32) for ky in range(3))
-            outer, inner = 0.5 * (g0 + g2), 0.5 * g1
-            u[0, at] = w[dz, 0, kx]
-            u[1, at] = (outer + inner).astype(BF16)
-            u[2, at] = (outer - inner).astype(BF16)
-            u[3, at] = w[dz, 2, kx]
-
-
-def four_rows(x):
+    for i, (w, u) in enumerate(((wa, ua), (wb, ub))):
+        chan = w.shape[3]
+        total = jnp.zeros((1, w.shape[4]), F32)
+        for kx in range(3):
+            for dz in range(3):
+                at = slice((3 * kx + dz) * chan, (3 * kx + dz + 1) * chan)
+                g0, g1, g2 = (w[dz, ky, kx].astype(F32) for ky in range(3))
+                outer, inner = 0.5 * (g0 + g2), 0.5 * g1
+                u[0, at] = w[dz, 0, kx]
+                u[1, at] = (outer + inner).astype(BF16)
+                u[2, at] = (outer - inner).astype(BF16)
+                u[3, at] = w[dz, 2, kx]
+                total = total + jnp.sum(outer + inner, axis=0, keepdims=True)
+        sums[i : i + 1] = total
+
+
+def four_rows(x, level):
     x = x.reshape((x.shape[0] // 2, 2) + x.shape[1:])
     even, odd = x[:, 0], x[:, 1]
-    return (even[:-1] - even[1:], odd[:-1] + even[1:], even[1:] - odd[:-1], odd[:-1] - odd[1:])
+    return (even[:-1] - even[1:], odd[:-1] + even[1:] - level, even[1:] - odd[:-1], odd[:-1] - odd[1:])
+
+
+def twice_mean(x):
+    x = x.astype(F32).reshape(-1, 8, x.shape[-1])
+    x = jnp.sum(jnp.sum(x, axis=0), axis=0, keepdims=True) * (2.0 / (x.shape[0] * 8 * x.shape[2]))
+    return jnp.sum(x, axis=1, keepdims=True)
 
 
 def cube_kernel(cfg, *refs):
     sources, zl, third_rows, vb, in_chan, mid_chan, out_chan, flip = cfg
     near, far = refs[: sources // 2], refs[sources // 2 : sources]
-    wa, ba, ub, bb, out, a3, mid, vm, ms = refs[sources:]
+    ua, ba, ub, bb, sums, out, va, mid, vm, ms = refs[sources:]
     me = lax.axis_index("gz")
     depth = sources * zl
     xs = 2 * vb
@@ -297,37 +306,24 @@
         [jnp.where((k_to == k_at) & (z_at == z_to + dz), 1.0, 0.0).astype(BF16) for dz in (-1, 0, 1)], axis=0
     )
     parts = 2 * tiles + 1
+    level_a = twice_mean(near[0][...])
     for vl in range(vb + 2):
+        y = []
         for c in range(parts):
             x = jnp.concatenate(
                 [part for k in range(sources // 2) for part in (near[k][(me % 2) * vb + vl, c], far[k][vl, c])], axis=0
             )
-            y = jnp.dot(gather, x, preferred_element_type=F32).astype(BF16).reshape(3, 8, depth, in_chan)
+            y.append(jnp.dot(gather, x, preferred_element_type=F32).reshape(3, 8, depth, in_chan))
+        for side in range(2):
             for dz in range(3):
-                lanes = slice(dz * in_chan, (dz + 1) * in_chan)
-                if c < 2 * tiles:
-                    x_at, y_at = 2 * vl + c // tiles, 2 + 8 * (c % tiles)
-                    a3[y_at : y_at + 8, x_at, :, lanes] = y[dz]
-                else:
-                    for side in range(2):
-                        a3[0:2, 2 * vl + side, :, lanes] = y[dz, 4 * side : 4 * side + 2]
-                        a3[third_rows + 2 : third_rows + 4, 2 * vl + side, :, lanes] = y[dz, 4 * side + 2 : 4 * side + 4]
-
-    taps = [(ky, kx) for ky in range(3) for kx in range(3)]
+                edge = y[parts - 1][dz, 4 * side : 4 * side + 4]
+                x = [edge[0:2]] + [y[side * tiles + i][dz] for i in range(tiles)] + [edge[2:4]]
+                for t, v in enumerate(four_rows(jnp.concatenate(x, axis=0), level_a)):
+                    va[t, :, 2 * vl + side, :, dz * in_chan : (dz + 1) * in_chan] = v.astype(BF16)
+
     mid_x = xs + 2
     mid_rows = third_rows + 2
-    step = 9 if mid_rows % 9 == 0 else 1
-
-    def iso_a(c, _):
-        first = c * step
-        n = step * mid_x * depth
-        x = jnp.concatenate([a3[pl.ds(first + ky, step), kx : kx + mid_x].reshape(n, 3 * in_chan) for ky, kx in taps], axis=1)
-        w = jnp.concatenate([wa[dz, ky, kx] for ky, kx in taps for dz in range(3)], axis=0)
-        y = jnp.maximum(jnp.dot(x, w, preferred_element_type=F32) + ba[...], 0.0)
-        mid[pl.ds(first, step)] = y.reshape(step, mid_x, depth, mid_chan).astype(BF16)
-        return 0
-
-    lax.fori_loop(0, mid_rows // step, iso_a, 0)
+    pairs_a = mid_rows // 2
 
     def products(v, u, first, count, breadth, chan):
         n = count * breadth * depth
@@ -338,6 +334,15 @@
         m1, m2 = ms[slot, 1, 0:n], ms[slot, 2, 0:n]
         return ms[slot, 0, 0:n] + (m1 + m2), (m1 - m2) - ms[slot, 3, 0:n]
 
+    step = 3 if pairs_a % 3 == 0 else 1
+    bias = ba[...] + level_a * sums[0:1]
+    for first in range(0, pairs_a, step):
+        ys = [jnp.maximum(y + bias, 0.0).astype(BF16) for y in products(va, ua, first, step, mid_x, in_chan)]
+        for i, y in enumerate(ys):
+            y = y.reshape(step, mid_x, depth, mid_chan)
+            for j in range(step):
+                mid[2 * (first + j) + i] = y[j]
+
     row, col = lax.axis_index("xy"), lax.axis_index("gz")
 
     @pl.when(row == 0)
@@ -357,6 +362,8 @@
         mid[:, mid_x - 1] = jnp.zeros(mid.shape[:1] + mid.shape[2:], BF16)
 
     pairs_b = third_rows // 2
+    level_b = twice_mean(mid[4:8])
+    bias = bb[...] + level_b * sums[1:2]
     step = 4 if pairs_b % 4 == 0 else 1
     if flip:
         n = xs * depth
@@ -366,12 +373,14 @@
     for first in range(0, pairs_b, step):
         for x_at in range(mid_x):
             x = mid[2 * first : 2 * (first + step) + 2, x_at].astype(F32)
-            for t, v in enumerate(four_rows(x)):
+            for t, v in enumerate(four_rows(x, level_b)):
                 here = v.shape
                 vm[t, first : first + step, x_at, :, mid_chan : 2 * mid_chan] = v.astype(BF16)
                 v = v.reshape(step, depth // 8, 8, mid_chan)
                 sub = lax.broadcasted_iota(jnp.int32, v.shape, 2)
                 none = jnp.zeros_like(v[:, :1])
+                if t == 1:
+                    none = none - level_b
                 rolled = pltpu.roll(v, 1, 2)
                 moved = jnp.where(sub == 0, jnp.concatenate([none, rolled[:, :-1]], axis=1), rolled)
                 vm[t, first : first + step, x_at, :, 0:mid_chan] = moved.reshape(here).astype(BF16)
@@ -379,7 +388,7 @@
                 moved = jnp.where(sub == 7, jnp.concatenate([rolled[:, 1:], none], axis=1), rolled)
                 vm[t, first : first + step, x_at, :, 2 * mid_chan :] = moved.reshape(here).astype(BF16)
         for i, y in enumerate(products(vm, ub, first, step, xs, mid_chan)):
-            y = jnp.maximum(y + bb[...], 0.0).astype(BF16)
+            y = jnp.maximum(y + bias, 0.0).astype(BF16)
             if flip:
                 y = y.reshape(step, xs * depth, out_chan)
                 for j in range(step):
@@ -423,20 +432,28 @@
     m = zl * period
     groups = width // 16 + 1
     parts = 2 * (third_rows // 8) + 1
+    def wide(x, count):
+        return jnp.pad(x, ((0, count - x.shape[0]), (0, 128 - x.shape[1])))
+
+    packed = jnp.concatenate(
+        [
+            jnp.transpose(weight_third, (2, 3, 1, 0)).reshape(576, 128),
+            wide(jnp.transpose(weight_second, (2, 3, 1, 0)).reshape(288, 64), 288),
+            wide(jnp.transpose(weight_first, (1, 2, 3, 0)).reshape(9, 32), 16),
+        ],
+        axis=0,
+    )
+    biases = jnp.concatenate([wide(x[None], 1) for x in (bias_first, bias_second, bias_third)] + [jnp.zeros((5, 128), F32)])
     banded = pl.pallas_call(
         weight_kernel,
         out_shape=jax.ShapeDtypeStruct((BIAS + 16, 256), BF16),
-        in_specs=[VMEM] * 6,
+        in_specs=[VMEM] * 2,
         out_specs=VMEM,
         scratch_shapes=[pltpu.VMEM((16, 128), F32)],
-        compiler_params=pltpu.CompilerParams(vmem_limit_bytes=60 << 20),
+        compiler_params=pltpu.CompilerParams(vmem_limit_bytes=20 << 20),
         cost_estimate=pl.CostEstimate(flops=2000000000, bytes_accessed=2000000, transcendentals=0),
         name="weights",
-    )(
-        jnp.transpose(weight_first, (1, 2, 3, 0))[0], bias_first[None],
-        jnp.transpose(weight_second, (2, 3, 1, 0)), bias_second[None],
-        jnp.transpose(weight_third, (2, 3, 1, 0)), bias_third[None],
-    )
+    )(packed, biases)
     chips = dests // 2
     send = pl.pallas_call(
         functools.partial(plane_kernel, (zl, rows, width, chips, 2 * vb)),
@@ -455,18 +472,20 @@
     )(first, raw_volume, second, banded)
     me = lax.axis_index("gz")
     other = (1 - me % 2) * vb
-    ub, own = pl.pallas_call(
+    kernels = (weight_iso_a, weight_iso_b)
+    ua, ub, sums, own = pl.pallas_call(
         filter_kernel,
-        out_shape=[
-            jax.ShapeDtypeStruct((4, 9 * weight_iso_b.shape[3], weight_iso_b.shape[4]), BF16),
+        out_shape=[jax.ShapeDtypeStruct((4, 9 * w.shape[3], w.shape[4]), BF16) for w in kernels]
+        + [
+            jax.ShapeDtypeStruct((2, weight_iso_b.shape[4]), F32),
             jax.ShapeDtypeStruct((vb + 2,) + send.shape[2:], BF16),
         ],
-        in_specs=[VMEM, VMEM],
-        out_specs=[VMEM, VMEM],
+        in_specs=[VMEM] * 3,
+        out_specs=[VMEM] * 4,
         compiler_params=pltpu.CompilerParams(vmem_limit_bytes=20 << 20),
         cost_estimate=pl.CostEstimate(flops=4000000000, bytes_accessed=8000000, transcendentals=0),
         name="filters",
-    )(send, weight_iso_b)
+    )(send, *kernels)
     near, far = [], []
     for k in range(chips):
         block = lax.dynamic_index_in_dim(send, (me // 2) ^ k, 0, keepdims=False)
@@ -484,17 +503,17 @@
     out = pl.pallas_call(
         functools.partial(cube_kernel, (dests, zl, third_rows, vb, in_chan, mid_chan, out_chan, flip)),
         out_shape=jax.ShapeDtypeStruct(shape, BF16),
-        in_specs=[VMEM] * (dests + 4),
+        in_specs=[VMEM] * (dests + 5),
         out_specs=VMEM,
         scratch_shapes=[
-            pltpu.VMEM((third_rows + 4, xs + 4, depth, 3 * in_chan), BF16),
+            pltpu.VMEM((4, third_rows // 2 + 1, xs + 4, depth, 3 * in_chan), BF16),
             pltpu.VMEM((third_rows + 2, xs + 2, depth, mid_chan), BF16),
             pltpu.VMEM((4, third_rows // 2, xs + 2, depth, 3 * mid_chan), BF16),
-            pltpu.VMEM((2, 4, 4 * xs * depth, mid_chan), F32),
+            pltpu.VMEM((2, 4, max(3 * (xs + 2), 4 * xs) * depth, mid_chan), F32),
         ],
         compiler_params=pltpu.CompilerParams(vmem_limit_bytes=(36 if depth <= 16 else 60) << 20),
         name="cubes",
-    )(*near, *far, weight_iso_a, bias_iso_a[None], ub, bias_iso_b[None])
+    )(*near, *far, ua, bias_iso_a[None], ub, bias_iso_b[None], sums)
     return out if flip else jnp.transpose(out, (2, 0, 1, 3))
 
 

time: 48.8 us -> 46.8 us (0.959)
  Pallas kernels: 27.2 us -> 24.1 us
  waiting for transfers between devices: 8.05 us -> 5.79 us
  other arithmetic: 0 us -> 1.73 us
  local copies, waits for them, and re-layouts: 2.39 us -> 3.88 us
    ppermute x3, waiting for transfers between devices: 7.07 us -> 4.81 us  [body(): block = lax.ppermute(block, 'gz', [(i, i ^ 2 * k) for i in range(dests)])]
    pallas_call x1, Pallas kernels: 2.46 us -> 0.27 us  [body(): pl.pallas_call(weight_kernel, out_shape=jax.ShapeDtypeStruct((BIAS + 16,...]
    concatenate x0 -> x2, other arithmetic: none -> 1.73 us  [the longest x1 0.97 us: body(): jnp.concatenate([jnp.transpose(weight_third, (2, 3, 1, 0)).reshape(576, 1...]
    pallas_call x1, Pallas kernels: 13.4 us -> 11.7 us  [body(): pl.pallas_call(functools.partial(cube_kernel, (dests, zl, third_rows, vb,...]
    pallas_call x1, Pallas kernels: 0.83 us -> 1.58 us  [body(): pl.pallas_call(filter_kernel, out_shape=[jax.ShapeDtypeStruct((4, 9 * w.s...]
    unnamed x12 -> x10, local copies, waits for them, and re-layouts: 1.38 us -> 2.08 us
    reshape x0 -> x1, local copies, waits for them, and re-layouts: none -> 0.7 us  [body(): jnp.transpose(weight_first, (1, 2, 3, 0)).reshape(9, 32)]
  transfers between devices with their start and end apart: 9 -> 9, of which waited for: 4 -> 4; matrix products, arithmetic and copies ran while one was open for 0% -> 5% of each run, Pallas kernels for 7% -> 4%
where the time goes in v3:
time: 46.8 us; the launch traced here: 46.5 us
  Pallas kernels  24.1 us (51%)
  starting transfers between devices  10.9 us (23%)
  waiting for transfers between devices  5.79 us (12%)
  local copies, waits for them, and re-layouts  3.88 us (8%)
  other arithmetic  1.73 us (4%)
    pallas_call x1, Pallas kernels, body(): pl.pallas_call(functools.partial(cube_kernel, (dests, zl, third_rows, vb,...  11.7 us
    pallas_call x1, Pallas kernels, body(): pl.pallas_call(functools.partial(plane_kernel, (zl, rows, width, chips, 2...  10.5 us
    ppermute x2, starting transfers between devices, swap(): lax.ppermute(edge, 'xy', [(i, i + 1) for i in pairs] + [(i + 1, i) for i...  6.56 us
    ppermute x3, waiting for transfers between devices, body(): block = lax.ppermute(block, 'gz', [(i, i ^ 2 * k) for i in range(dests)])  4.81 us
    ppermute x3, starting transfers between devices, body(): block = lax.ppermute(block, 'gz', [(i, i ^ 2 * k) for i in range(dests)])  3.55 us
    unnamed x10, local copies, waits for them, and re-layouts  2.08 us
    pallas_call x1, Pallas kernels, body(): pl.pallas_call(filter_kernel, out_shape=[jax.ShapeDtypeStruct((4, 9 * w.s...  1.58 us
    ppermute x4, waiting for transfers between devices, body(): far.append(lax.ppermute(window, 'gz', [(i, i ^ 1) for i in range(dests)]))  0.97 us
  transfers between devices with their start and end apart: 9, of which 4 were waited for; matrix products, arithmetic and copies ran while one was open for 5% of the time, Pallas kernels for 4%

profile of v3, /device:TPU:0, one launch (start us, length us, event | category | flops | bytes accessed | tf_op | source)
XLA Modules:
  0.0 46.5 jit_solution(8387202858633903125)
XLA Ops:
  0.0 0.8 %constant_dynamic-slice_fusion.3 = (bf16[2,24,512]{2,1,0:T(8,128)(2,1)S(1)}, bf16[2,24,512]{2,1,0:T(8,128)(2,1)S(1)}) fusion(bf16[2,128,512]{2,1,0:T(8,128)(2,1)} %raw.1, s32[]{:T(128)S(6)} %select_n.47, s32[]{:T(128)S(6)} %select_n.46), kind=kLoop, calls=%fused_computation.22 | loop fusion | bytes 196616 | tf_op jit(solution)/shard_map/dynamic_slice | solution.py:425
  0.8 0.7 %collective-permute-start.1 = (bf16[2,24,512]{2,1,0:T(8,128)(2,1)S(1)}, bf16[2,24,512]{2,1,0:T(8,128)(2,1)S(1)}, u32[]{:S(2)}, u32[]{:S(2)}) collective-permute-start(bf16[2,24,512]{2,1,0:T(8,128)(2,1)S(1)} %get-tuple-element.17), channel_id=1, source_target_pairs={{1,2},{2,1},{5,6},{6,5},{9,10},{10,9},{13,14},{14,13},{17,18},{18,... | collective-permute-start | bytes 147464 | tf_op jit(solution)/shard_map/ppermute | solution.py:426
  1.5 5.9 %collective-permute-start = (bf16[2,24,512]{2,1,0:T(8,128)(2,1)S(1)}, bf16[2,24,512]{2,1,0:T(8,128)(2,1)S(1)}, u32[]{:S(2)}, u32[]{:S(2)}) collective-permute-start(bf16[2,24,512]{2,1,0:T(8,128)(2,1)S(1)} %get-tuple-element.18), channel_id=1, source_target_pairs={{0,1},{2,3},{1,0},{3,2},{4,5},{6,7},{5,4},{7,6},{8,9},{10,11},{9,8... | collective-permute-start | bytes 147464 | tf_op jit(solution)/shard_map/ppermute | solution.py:426
  7.4 0.7 %reshape.11 = bf16[9,32]{1,0:T(8,128)(2,1)S(1)} reshape(bf16[1,3,3,32]{3,2,1,0:T(4,128)(2,1)} %bitcast.24) | data formatting | bytes 1152 | tf_op jit(solution)/shard_map/reshape | solution.py:442
  8.1 0.1 pad.23.clone
  8.2 1.0 %fusion.4.packed = bf16[880,128]{1,0:T(8,128)(2,1)S(1)} fusion(bf16[9,32]{1,0:T(8,128)(2,1)S(1)} %reshape.11, bf16[288,64]{1,0:T(8,128)(2,1)} %bitcast.23, bf16[576,128]{1,0:T(8,128)(2,1)} %bitcast.22), kind=kLoop, calls=%fused_computation.7 | loop fusion | flops 1351680 | bytes 410176 | tf_op jit(solution)/shard_map/concatenate | solution.py:438
  9.2 0.8 %fusion.6.biases = f32[8,128]{1,0:T(8,128)S(1)} fusion(f32[1,64]{1,0:T(1,128)} %bitcast.25, f32[1,32]{1,0:T(1,128)} %bitcast.26, f32[1,128]{1,0:T(1,128)} %bitcast.27, f32[8]{0:T(128)S(1)} %pad.23.clone), kind=kLoop, calls=%fused_computation.16 | loop fusion | flops 9216 | bytes 5024 | tf_op jit(solution)/shard_map/concatenate | solution.py:446
  9.9 0.3 weights.1.banded
  10.3 0.6 %copy-done = bf16[2,128,512]{2,1,0:T(8,128)(2,1)S(1)} copy-done((bf16[2,128,512]{2,1,0:T(8,128)(2,1)S(1)}, bf16[2,128,512]{2,1,0:T(8,128)(2,1)}, u32[]{:S(2)}) %copy-start) | copy-done | bytes 262168
  10.9 10.5 %planes.1.send = bf16[4,10,5,16,128]{4,3,2,1,0:T(8,128)(2,1)S(1)} custom-call(bf16[2,24,512]{2,1,0:T(8,128)(2,1)S(1)} %collective-permute-done.swap_a, bf16[2,128,512]{2,1,0:T(8,128)(2,1)S(1)} %copy-done, bf16[2,24,512]{2,1,0:T(8,128)(2,1)S(1)} %collective-permute-done.1.swap_b, bf16[2832,256]{1,0:T(8,128)(2,1)S(1)} %weights.1.banded), custom_call_target="tpu_custom_call" | custom-call | tf_op jit(solution)/shard_map/planes/pallas_call | solution.py:458
  21.4 0.2 dynamic-slice_bitcast_fusion
  21.6 2.5 %collective-permute-start.4 = (bf16[10,5,16,128]{3,2,1,0:T(8,128)(2,1)S(1)}, bf16[10,5,16,128]{3,2,1,0:T(8,128)(2,1)S(1)}, u32[]{:S(2)}, u32[]{:S(2)}) collective-permute-start(bf16[10,5,16,128]{3,2,1,0:T(8,128)(2,1)S(1)} %get-tuple-element.13), channel_id=1, source_target_pairs={{0,24},{4,28},{8,16},{12,20},{16,8},{20,12},{24,0},{28,4},{1,25},{... | collective-permute-start | bytes 614408 | tf_op jit(solution)/shard_map/ppermute | solution.py:493
  24.1 0.5 %collective-permute-start.3 = (bf16[10,5,16,128]{3,2,1,0:T(8,128)(2,1)S(1)}, bf16[10,5,16,128]{3,2,1,0:T(8,128)(2,1)S(1)}, u32[]{:S(2)}, u32[]{:S(2)}) collective-permute-start(bf16[10,5,16,128]{3,2,1,0:T(8,128)(2,1)S(1)} %get-tuple-element.14), channel_id=1, source_target_pairs={{0,16},{4,20},{8,24},{12,28},{16,0},{20,4},{24,8},{28,12},{1,17},{... | collective-permute-start | bytes 614408 | tf_op jit(solution)/shard_map/ppermute | solution.py:493
  24.6 0.5 %collective-permute-start.2 = (bf16[10,5,16,128]{3,2,1,0:T(8,128)(2,1)S(1)}, bf16[10,5,16,128]{3,2,1,0:T(8,128)(2,1)S(1)}, u32[]{:S(2)}, u32[]{:S(2)}) collective-permute-start(bf16[10,5,16,128]{3,2,1,0:T(8,128)(2,1)S(1)} %get-tuple-element.15), channel_id=1, source_target_pairs={{0,8},{4,12},{8,0},{12,4},{16,24},{20,28},{24,16},{28,20},{1,9},{5... | collective-permute-start | bytes 614408 | tf_op jit(solution)/shard_map/ppermute | solution.py:493
  25.1 1.5 %copy-done.4 = bf16[3,3,3,128,256]{4,3,2,1,0:T(8,128)(2,1)S(1)} copy-done((bf16[3,3,3,128,256]{4,3,2,1,0:T(8,128)(2,1)S(1)}, bf16[3,3,3,128,256]{4,3,2,1,0:T(8,128)(2,1)}, u32[]{:S(2)}) %copy-start.4) | copy-done | bytes 1769496
  26.6 1.6 %filters.1 = (bf16[4,1152,256]{2,1,0:T(8,128)(2,1)S(1)}, bf16[4,2304,256]{2,1,0:T(8,128)(2,1)S(1)}, f32[2,256]{1,0:T(2,128)S(1)}, bf16[6,5,16,128]{3,2,1,0:T(8,128)(2,1)S(1)}) custom-call(bf16[4,10,5,16,128]{4,3,2,1,0:T(8,128)(2,1)S(1)} %planes.1.send, bf16[3,3,3,128,256]{4,3,2,1,0:T(8,128)(2,1)S(1)} %copy-done.4, bf16[3,3,3,256,256]{4,3,2,1,0:T(8,128)(2,1)S(1)} %copy-done.3), custom_call_target="tpu_custom_call" | custom-call | flops 4000000000 | bytes 8000000 | tf_op jit(solution)/shard_map/filters/pallas_call | solution.py:476
  28.2 0.1 collective-permute-start.5
  28.3 2.3 %collective-permute-done.4.refs_3_ = bf16[10,5,16,128]{3,2,1,0:T(8,128)(2,1)S(1)} collective-permute-done((bf16[10,5,16,128]{3,2,1,0:T(8,128)(2,1)S(1)}, bf16[10,5,16,128]{3,2,1,0:T(8,128)(2,1)S(1)}, u32[]{:S(2)}, u32[]{:S(2)}) %collective-permute-start.4) | collective-permute-done | bytes 204832 | tf_op jit(solution)/shard_map/ppermute | solution.py:493
  30.6 0.1 collective-permute-start.8
  30.6 2.5 %collective-permute-done.3.refs_2_ = bf16[10,5,16,128]{3,2,1,0:T(8,128)(2,1)S(1)} collective-permute-done((bf16[10,5,16,128]{3,2,1,0:T(8,128)(2,1)S(1)}, bf16[10,5,16,128]{3,2,1,0:T(8,128)(2,1)S(1)}, u32[]{:S(2)}, u32[]{:S(2)}) %collective-permute-start.3) | collective-permute-done | bytes 204832 | tf_op jit(solution)/shard_map/ppermute | solution.py:493
  33.3 0.5 %collective-permute-start.6 = (bf16[6,5,16,128]{3,2,1,0:T(8,128)(2,1)S(1)}, bf16[6,5,16,128]{3,2,1,0:T(8,128)(2,1)S(1)}, u32[]{:S(2)}, u32[]{:S(2)}) collective-permute-start(bf16[6,5,16,128]{3,2,1,0:T(8,128)(2,1)S(1)} %constant_dynamic-slice_fusion.2), channel_id=1, source_target_pairs={{0,4},{4,0},{8,12},{12,8},{16,20},{20,16},{24,28},{28,24},{1,5},{5... | collective-permute-start | bytes 368648 | tf_op jit(solution)/shard_map/ppermute | solution.py:496
  33.8 0.7 %collective-permute-done.7.refs_6_ = bf16[6,5,16,128]{3,2,1,0:T(8,128)(2,1)S(1)} collective-permute-done((bf16[6,5,16,128]{3,2,1,0:T(8,128)(2,1)S(1)}, bf16[6,5,16,128]{3,2,1,0:T(8,128)(2,1)S(1)}, u32[]{:S(2)}, u32[]{:S(2)}) %collective-permute-start.7) | collective-permute-done | bytes 122912 | tf_op jit(solution)/shard_map/ppermute | solution.py:496
  34.6 0.2 collective-permute-done.6.refs_5_
  34.8 11.7 %cubes.1 = bf16[16,16,8,256]{3,2,1,0:T(8,128)(2,1)} custom-call(bf16[10,5,16,128]{3,2,1,0:T(8,128)(2,1)S(1)} %get-tuple-element.16.refs_0_, bf16[10,5,16,128]{3,2,1,0:T(8,128)(2,1)S(1)} %collective-permute-done.2.refs_1_, bf16[10,5,16,128]{3,2,1,0:T(8,128)(2,1)S(1)} %collective-permute-done.3.refs_2_, ...), custom_call_target="tpu_custom_call" | custom-call | tf_op jit(solution)/shard_map/cubes/pallas_call | solution.py:503
  (18 shorter events, 0.1 us)
Async XLA Ops:
  0.8 9.4 %collective-permute-start.1 = (bf16[2,24,512]{2,1,0:T(8,128)(2,1)S(1)}, bf16[2,24,512]{2,1,0:T(8,128)(2,1)S(1)}, u32[]{:S(2)}, u32[]{:S(2)}) collective-permute-start(bf16[2,24,512]{2,1,0:T(8,128)(2,1)S(1)} %get-tuple-element.17), channel_id=1, source_target_pairs={{1,2},{2,1},{5,6},{6,5},{9,10},{10,9},{13,14},{14,13},{17,18},{18,... | collective-permute-start | bytes 147464 | tf_op jit(solution)/shard_map/ppermute | solution.py:426
  1.5 8.8 %collective-permute-start = (bf16[2,24,512]{2,1,0:T(8,128)(2,1)S(1)}, bf16[2,24,512]{2,1,0:T(8,128)(2,1)S(1)}, u32[]{:S(2)}, u32[]{:S(2)}) collective-permute-start(bf16[2,24,512]{2,1,0:T(8,128)(2,1)S(1)} %get-tuple-element.18), channel_id=1, source_target_pairs={{0,1},{2,3},{1,0},{3,2},{4,5},{6,7},{5,4},{7,6},{8,9},{10,11},{9,8... | collective-permute-start | bytes 147464 | tf_op jit(solution)/shard_map/ppermute | solution.py:426
  9.9 0.9 %copy-start = (bf16[2,128,512]{2,1,0:T(8,128)(2,1)S(1)}, bf16[2,128,512]{2,1,0:T(8,128)(2,1)}, u32[]{:S(2)}) copy-start(bf16[2,128,512]{2,1,0:T(8,128)(2,1)} %raw.1) | copy-start | bytes 786436
  10.2 14.9 %copy-start.3 = (bf16[3,3,3,256,256]{4,3,2,1,0:T(8,128)(2,1)S(1)}, bf16[3,3,3,256,256]{4,3,2,1,0:T(8,128)(2,1)}, u32[]{:S(2)}) copy-start(bf16[3,3,3,256,256]{4,3,2,1,0:T(8,128)(2,1)} %wb.1) | copy-start | bytes 10616836
  21.6 9.0 %collective-permute-start.4 = (bf16[10,5,16,128]{3,2,1,0:T(8,128)(2,1)S(1)}, bf16[10,5,16,128]{3,2,1,0:T(8,128)(2,1)S(1)}, u32[]{:S(2)}, u32[]{:S(2)}) collective-permute-start(bf16[10,5,16,128]{3,2,1,0:T(8,128)(2,1)S(1)} %get-tuple-element.13), channel_id=1, source_target_pairs={{0,24},{4,28},{8,16},{12,20},{16,8},{20,12},{24,0},{28,4},{1,25},{... | collective-permute-start | bytes 614408 | tf_op jit(solution)/shard_map/ppermute | solution.py:493
  24.1 9.1 %collective-permute-start.3 = (bf16[10,5,16,128]{3,2,1,0:T(8,128)(2,1)S(1)}, bf16[10,5,16,128]{3,2,1,0:T(8,128)(2,1)S(1)}, u32[]{:S(2)}, u32[]{:S(2)}) collective-permute-start(bf16[10,5,16,128]{3,2,1,0:T(8,128)(2,1)S(1)} %get-tuple-element.14), channel_id=1, source_target_pairs={{0,16},{4,20},{8,24},{12,28},{16,0},{20,4},{24,8},{28,12},{1,17},{... | collective-permute-start | bytes 614408 | tf_op jit(solution)/shard_map/ppermute | solution.py:493
  24.6 10.2 %copy-start.1 = (f32[256]{0:T(256)S(1)}, f32[256]{0:T(256)}, u32[]{:S(2)}) copy-start(f32[256]{0:T(256)} %param.19) | copy-start | bytes 3076
  24.6 10.2 %copy-start.2 = (f32[256]{0:T(256)S(1)}, f32[256]{0:T(256)}, u32[]{:S(2)}) copy-start(f32[256]{0:T(256)} %param.21) | copy-start | bytes 3076
  24.6 8.7 %collective-permute-start.2 = (bf16[10,5,16,128]{3,2,1,0:T(8,128)(2,1)S(1)}, bf16[10,5,16,128]{3,2,1,0:T(8,128)(2,1)S(1)}, u32[]{:S(2)}, u32[]{:S(2)}) collective-permute-start(bf16[10,5,16,128]{3,2,1,0:T(8,128)(2,1)S(1)} %get-tuple-element.15), channel_id=1, source_target_pairs={{0,8},{4,12},{8,0},{12,4},{16,24},{20,28},{24,16},{28,20},{1,9},{5... | collective-permute-start | bytes 614408 | tf_op jit(solution)/shard_map/ppermute | solution.py:493
  25.1 1.5 %copy-start.4 = (bf16[3,3,3,128,256]{4,3,2,1,0:T(8,128)(2,1)S(1)}, bf16[3,3,3,128,256]{4,3,2,1,0:T(8,128)(2,1)}, u32[]{:S(2)}) copy-start(bf16[3,3,3,128,256]{4,3,2,1,0:T(8,128)(2,1)} %wa.1) | copy-start | bytes 5308420
  28.2 5.7 %collective-permute-start.5 = (bf16[6,5,16,128]{3,2,1,0:T(8,128)(2,1)S(1)}, bf16[6,5,16,128]{3,2,1,0:T(8,128)(2,1)S(1)}, u32[]{:S(2)}, u32[]{:S(2)}) collective-permute-start(bf16[6,5,16,128]{3,2,1,0:T(8,128)(2,1)S(1)} %get-tuple-element.9), channel_id=1, source_target_pairs={{0,4},{4,0},{8,12},{12,8},{16,20},{20,16},{24,28},{28,24},{1,5},{5... | collective-permute-start | bytes 368648 | tf_op jit(solution)/shard_map/ppermute | solution.py:496
  30.6 3.3 %collective-permute-start.8 = (bf16[6,5,16,128]{3,2,1,0:T(8,128)(2,1)S(1)}, bf16[6,5,16,128]{3,2,1,0:T(8,128)(2,1)S(1)}, u32[]{:S(2)}, u32[]{:S(2)}) collective-permute-start(bf16[6,5,16,128]{3,2,1,0:T(8,128)(2,1)S(1)} %constant_dynamic-slice_fusion), channel_id=1, source_target_pairs={{0,4},{4,0},{8,12},{12,8},{16,20},{20,16},{24,28},{28,24},{1,5},{5... | collective-permute-start | bytes 368648 | tf_op jit(solution)/shard_map/ppermute | solution.py:496
  33.2 1.4 %collective-permute-start.7 = (bf16[6,5,16,128]{3,2,1,0:T(8,128)(2,1)S(1)}, bf16[6,5,16,128]{3,2,1,0:T(8,128)(2,1)S(1)}, u32[]{:S(2)}, u32[]{:S(2)}) collective-permute-start(bf16[6,5,16,128]{3,2,1,0:T(8,128)(2,1)S(1)} %constant_dynamic-slice_fusion.1), channel_id=1, source_target_pairs={{0,4},{4,0},{8,12},{12,8},{16,20},{20,16},{24,28},{28,24},{1,5},{5... | collective-permute-start | bytes 368648 | tf_op jit(solution)/shard_map/ppermute | solution.py:496
  33.3 1.5 %collective-permute-start.6 = (bf16[6,5,16,128]{3,2,1,0:T(8,128)(2,1)S(1)}, bf16[6,5,16,128]{3,2,1,0:T(8,128)(2,1)S(1)}, u32[]{:S(2)}, u32[]{:S(2)}) collective-permute-start(bf16[6,5,16,128]{3,2,1,0:T(8,128)(2,1)S(1)} %constant_dynamic-slice_fusion.2), channel_id=1, source_target_pairs={{0,4},{4,0},{8,12},{12,8},{16,20},{20,16},{24,28},{28,24},{1,5},{5... | collective-permute-start | bytes 368648 | tf_op jit(solution)/shard_map/ppermute | solution.py:496

commit v4 on v3

--- a/solution.py
+++ b/solution.py
@@ -39,7 +39,7 @@
     return x + pltpu.roll(x, 32, 1) + pltpu.roll(x, 64, 1) + pltpu.roll(x, 96, 1)
 
 
-def weight_kernel(packed, biases, banded, small):
+def weight_kernel(packed, biases, raw, banded, small):
     small[0:16] = packed[864:880].astype(F32)
     small[9:11] = biases[0:2]
     tap = []
@@ -447,13 +447,13 @@
     banded = pl.pallas_call(
         weight_kernel,
         out_shape=jax.ShapeDtypeStruct((BIAS + 16, 256), BF16),
-        in_specs=[VMEM] * 2,
+        in_specs=[VMEM] * 3,
         out_specs=VMEM,
         scratch_shapes=[pltpu.VMEM((16, 128), F32)],
         compiler_params=pltpu.CompilerParams(vmem_limit_bytes=20 << 20),
         cost_estimate=pl.CostEstimate(flops=2000000000, bytes_accessed=2000000, transcendentals=0),
         name="weights",
-    )(packed, biases)
+    )(packed, biases, raw_volume)
     chips = dests // 2
     send = pl.pallas_call(
         functools.partial(plane_kernel, (zl, rows, width, chips, 2 * vb)),

time: 46.8 us -> 47.7 us (1.019)
  local copies, waits for them, and re-layouts: 3.88 us -> 4.83 us
    unnamed x10 -> x12, local copies, waits for them, and re-layouts: 2.08 us -> 3.03 us
where the time goes in v4:
time: 47.7 us; the launch traced here: 47.5 us
  Pallas kernels  24 us (50%)
  starting transfers between devices  10.9 us (23%)
  waiting for transfers between devices  5.82 us (12%)
  local copies, waits for them, and re-layouts  4.83 us (10%)
  other arithmetic  1.73 us (4%)
    pallas_call x1, Pallas kernels, body(): pl.pallas_call(functools.partial(cube_kernel, (dests, zl, third_rows, vb,...  11.7 us
    pallas_call x1, Pallas kernels, body(): pl.pallas_call(functools.partial(plane_kernel, (zl, rows, width, chips, 2...  10.5 us
    ppermute x2, starting transfers between devices, swap(): lax.ppermute(edge, 'xy', [(i, i + 1) for i in pairs] + [(i + 1, i) for i...  6.56 us
    ppermute x3, waiting for transfers between devices, body(): block = lax.ppermute(block, 'gz', [(i, i ^ 2 * k) for i in range(dests)])  4.84 us
    ppermute x3, starting transfers between devices, body(): block = lax.ppermute(block, 'gz', [(i, i ^ 2 * k) for i in range(dests)])  3.55 us
    unnamed x12, local copies, waits for them, and re-layouts  3.03 us
    pallas_call x1, Pallas kernels, body(): pl.pallas_call(filter_kernel, out_shape=[jax.ShapeDtypeStruct((4, 9 * w.s...  1.58 us
    ppermute x4, waiting for transfers between devices, body(): far.append(lax.ppermute(window, 'gz', [(i, i ^ 1) for i in range(dests)]))  0.97 us
  transfers between devices with their start and end apart: 9, of which 4 were waited for; matrix products, arithmetic and copies ran while one was open for 5% of the time, Pallas kernels for 4%

profile of v4, /device:TPU:0, one launch (start us, length us, event | category | flops | bytes accessed | tf_op | source)
XLA Modules:
  0.0 47.5 jit_solution(11301946604066426621)
XLA Ops:
  0.0 0.8 %constant_dynamic-slice_fusion.3 = (bf16[2,24,512]{2,1,0:T(8,128)(2,1)S(1)}, bf16[2,24,512]{2,1,0:T(8,128)(2,1)S(1)}) fusion(bf16[2,128,512]{2,1,0:T(8,128)(2,1)} %raw.3, s32[]{:T(128)S(6)} %select_n.47, s32[]{:T(128)S(6)} %select_n.46), kind=kLoop, calls=%fused_computation.22 | loop fusion | bytes 196616 | tf_op jit(solution)/shard_map/dynamic_slice | solution.py:425
  0.8 0.7 %collective-permute-start.1 = (bf16[2,24,512]{2,1,0:T(8,128)(2,1)S(1)}, bf16[2,24,512]{2,1,0:T(8,128)(2,1)S(1)}, u32[]{:S(2)}, u32[]{:S(2)}) collective-permute-start(bf16[2,24,512]{2,1,0:T(8,128)(2,1)S(1)} %get-tuple-element.17), channel_id=1, source_target_pairs={{1,2},{2,1},{5,6},{6,5},{9,10},{10,9},{13,14},{14,13},{17,18},{18,... | collective-permute-start | bytes 147464 | tf_op jit(solution)/shard_map/ppermute | solution.py:426
  1.5 5.9 %collective-permute-start = (bf16[2,24,512]{2,1,0:T(8,128)(2,1)S(1)}, bf16[2,24,512]{2,1,0:T(8,128)(2,1)S(1)}, u32[]{:S(2)}, u32[]{:S(2)}) collective-permute-start(bf16[2,24,512]{2,1,0:T(8,128)(2,1)S(1)} %get-tuple-element.18), channel_id=1, source_target_pairs={{0,1},{2,3},{1,0},{3,2},{4,5},{6,7},{5,4},{7,6},{8,9},{10,11},{9,8... | collective-permute-start | bytes 147464 | tf_op jit(solution)/shard_map/ppermute | solution.py:426
  7.4 0.7 %reshape.11 = bf16[9,32]{1,0:T(8,128)(2,1)S(1)} reshape(bf16[1,3,3,32]{3,2,1,0:T(4,128)(2,1)} %bitcast.24) | data formatting | bytes 1152 | tf_op jit(solution)/shard_map/reshape | solution.py:442
  8.1 0.1 pad.23.clone
  8.2 1.0 %fusion.4.packed = bf16[880,128]{1,0:T(8,128)(2,1)S(1)} fusion(bf16[9,32]{1,0:T(8,128)(2,1)S(1)} %reshape.11, bf16[288,64]{1,0:T(8,128)(2,1)} %bitcast.23, bf16[576,128]{1,0:T(8,128)(2,1)} %bitcast.22), kind=kLoop, calls=%fused_computation.7 | loop fusion | flops 1351680 | bytes 410176 | tf_op jit(solution)/shard_map/concatenate | solution.py:438
  9.2 0.8 %fusion.6.biases = f32[8,128]{1,0:T(8,128)S(1)} fusion(f32[1,64]{1,0:T(1,128)} %bitcast.25, f32[1,32]{1,0:T(1,128)} %bitcast.26, f32[1,128]{1,0:T(1,128)} %bitcast.27, f32[8]{0:T(128)S(1)} %pad.23.clone), kind=kLoop, calls=%fused_computation.16 | loop fusion | flops 9216 | bytes 5024 | tf_op jit(solution)/shard_map/concatenate | solution.py:446
  9.9 0.9 %copy-done = bf16[2,128,512]{2,1,0:T(8,128)(2,1)S(1)} copy-done((bf16[2,128,512]{2,1,0:T(8,128)(2,1)S(1)}, bf16[2,128,512]{2,1,0:T(8,128)(2,1)}, u32[]{:S(2)}) %copy-start) | copy-done | bytes 262168
  10.9 0.3 weights.1.banded
  11.2 0.6 %copy-done.1 = bf16[2,128,512]{2,1,0:T(8,128)(2,1)S(1)} copy-done((bf16[2,128,512]{2,1,0:T(8,128)(2,1)S(1)}, bf16[2,128,512]{2,1,0:T(8,128)(2,1)}, u32[]{:S(2)}) %copy-start.1) | copy-done | bytes 262168
  11.8 10.5 %planes.1.send = bf16[4,10,5,16,128]{4,3,2,1,0:T(8,128)(2,1)S(1)} custom-call(bf16[2,24,512]{2,1,0:T(8,128)(2,1)S(1)} %collective-permute-done.swap_a, bf16[2,128,512]{2,1,0:T(8,128)(2,1)S(1)} %copy-done.1, bf16[2,24,512]{2,1,0:T(8,128)(2,1)S(1)} %collective-permute-done.1.swap_b, bf16[2832,256]{1,0:T(8,128)(2,1)S(1)} %weights.1.banded), custom_call_target="tpu_custom_call" | custom-call | tf_op jit(solution)/shard_map/planes/pallas_call | solution.py:458
  22.3 0.2 dynamic-slice_bitcast_fusion
  22.5 2.5 %collective-permute-start.4 = (bf16[10,5,16,128]{3,2,1,0:T(8,128)(2,1)S(1)}, bf16[10,5,16,128]{3,2,1,0:T(8,128)(2,1)S(1)}, u32[]{:S(2)}, u32[]{:S(2)}) collective-permute-start(bf16[10,5,16,128]{3,2,1,0:T(8,128)(2,1)S(1)} %get-tuple-element.13), channel_id=1, source_target_pairs={{0,24},{4,28},{8,16},{12,20},{16,8},{20,12},{24,0},{28,4},{1,25},{... | collective-permute-start | bytes 614408 | tf_op jit(solution)/shard_map/ppermute | solution.py:493
  25.0 0.5 %collective-permute-start.3 = (bf16[10,5,16,128]{3,2,1,0:T(8,128)(2,1)S(1)}, bf16[10,5,16,128]{3,2,1,0:T(8,128)(2,1)S(1)}, u32[]{:S(2)}, u32[]{:S(2)}) collective-permute-start(bf16[10,5,16,128]{3,2,1,0:T(8,128)(2,1)S(1)} %get-tuple-element.14), channel_id=1, source_target_pairs={{0,16},{4,20},{8,24},{12,28},{16,0},{20,4},{24,8},{28,12},{1,17},{... | collective-permute-start | bytes 614408 | tf_op jit(solution)/shard_map/ppermute | solution.py:493
  25.5 0.5 %collective-permute-start.2 = (bf16[10,5,16,128]{3,2,1,0:T(8,128)(2,1)S(1)}, bf16[10,5,16,128]{3,2,1,0:T(8,128)(2,1)S(1)}, u32[]{:S(2)}, u32[]{:S(2)}) collective-permute-start(bf16[10,5,16,128]{3,2,1,0:T(8,128)(2,1)S(1)} %get-tuple-element.15), channel_id=1, source_target_pairs={{0,8},{4,12},{8,0},{12,4},{16,24},{20,28},{24,16},{28,20},{1,9},{5... | collective-permute-start | bytes 614408 | tf_op jit(solution)/shard_map/ppermute | solution.py:493
  26.1 1.5 %copy-done.5 = bf16[3,3,3,128,256]{4,3,2,1,0:T(8,128)(2,1)S(1)} copy-done((bf16[3,3,3,128,256]{4,3,2,1,0:T(8,128)(2,1)S(1)}, bf16[3,3,3,128,256]{4,3,2,1,0:T(8,128)(2,1)}, u32[]{:S(2)}) %copy-start.5) | copy-done | bytes 1769496
  27.5 1.6 %filters.1 = (bf16[4,1152,256]{2,1,0:T(8,128)(2,1)S(1)}, bf16[4,2304,256]{2,1,0:T(8,128)(2,1)S(1)}, f32[2,256]{1,0:T(2,128)S(1)}, bf16[6,5,16,128]{3,2,1,0:T(8,128)(2,1)S(1)}) custom-call(bf16[4,10,5,16,128]{4,3,2,1,0:T(8,128)(2,1)S(1)} %planes.1.send, bf16[3,3,3,128,256]{4,3,2,1,0:T(8,128)(2,1)S(1)} %copy-done.5, bf16[3,3,3,256,256]{4,3,2,1,0:T(8,128)(2,1)S(1)} %copy-done.4), custom_call_target="tpu_custom_call" | custom-call | flops 4000000000 | bytes 8000000 | tf_op jit(solution)/shard_map/filters/pallas_call | solution.py:476
  29.1 0.1 collective-permute-start.5
  29.2 2.3 %collective-permute-done.4.refs_3_ = bf16[10,5,16,128]{3,2,1,0:T(8,128)(2,1)S(1)} collective-permute-done((bf16[10,5,16,128]{3,2,1,0:T(8,128)(2,1)S(1)}, bf16[10,5,16,128]{3,2,1,0:T(8,128)(2,1)S(1)}, u32[]{:S(2)}, u32[]{:S(2)}) %collective-permute-start.4) | collective-permute-done | bytes 204832 | tf_op jit(solution)/shard_map/ppermute | solution.py:493
  31.6 2.6 %collective-permute-done.3.refs_2_ = bf16[10,5,16,128]{3,2,1,0:T(8,128)(2,1)S(1)} collective-permute-done((bf16[10,5,16,128]{3,2,1,0:T(8,128)(2,1)S(1)}, bf16[10,5,16,128]{3,2,1,0:T(8,128)(2,1)S(1)}, u32[]{:S(2)}, u32[]{:S(2)}) %collective-permute-start.3) | collective-permute-done | bytes 204832 | tf_op jit(solution)/shard_map/ppermute | solution.py:493
  34.3 0.5 %collective-permute-start.6 = (bf16[6,5,16,128]{3,2,1,0:T(8,128)(2,1)S(1)}, bf16[6,5,16,128]{3,2,1,0:T(8,128)(2,1)S(1)}, u32[]{:S(2)}, u32[]{:S(2)}) collective-permute-start(bf16[6,5,16,128]{3,2,1,0:T(8,128)(2,1)S(1)} %constant_dynamic-slice_fusion.2), channel_id=1, source_target_pairs={{0,4},{4,0},{8,12},{12,8},{16,20},{20,16},{24,28},{28,24},{1,5},{5... | collective-permute-start | bytes 368648 | tf_op jit(solution)/shard_map/ppermute | solution.py:496
  34.8 0.7 %collective-permute-done.7.refs_6_ = bf16[6,5,16,128]{3,2,1,0:T(8,128)(2,1)S(1)} collective-permute-done((bf16[6,5,16,128]{3,2,1,0:T(8,128)(2,1)S(1)}, bf16[6,5,16,128]{3,2,1,0:T(8,128)(2,1)S(1)}, u32[]{:S(2)}, u32[]{:S(2)}) %collective-permute-start.7) | collective-permute-done | bytes 122912 | tf_op jit(solution)/shard_map/ppermute | solution.py:496
  35.5 0.2 collective-permute-done.6.refs_5_
  35.8 11.7 %cubes.1 = bf16[16,16,8,256]{3,2,1,0:T(8,128)(2,1)} custom-call(bf16[10,5,16,128]{3,2,1,0:T(8,128)(2,1)S(1)} %get-tuple-element.16.refs_0_, bf16[10,5,16,128]{3,2,1,0:T(8,128)(2,1)S(1)} %collective-permute-done.2.refs_1_, bf16[10,5,16,128]{3,2,1,0:T(8,128)(2,1)S(1)} %collective-permute-done.3.refs_2_, ...), custom_call_target="tpu_custom_call" | custom-call | tf_op jit(solution)/shard_map/cubes/pallas_call | solution.py:503
  (20 shorter events, 0.2 us)
Async XLA Ops:
  0.8 10.4 %collective-permute-start.1 = (bf16[2,24,512]{2,1,0:T(8,128)(2,1)S(1)}, bf16[2,24,512]{2,1,0:T(8,128)(2,1)S(1)}, u32[]{:S(2)}, u32[]{:S(2)}) collective-permute-start(bf16[2,24,512]{2,1,0:T(8,128)(2,1)S(1)} %get-tuple-element.17), channel_id=1, source_target_pairs={{1,2},{2,1},{5,6},{6,5},{9,10},{10,9},{13,14},{14,13},{17,18},{18,... | collective-permute-start | bytes 147464 | tf_op jit(solution)/shard_map/ppermute | solution.py:426
  1.5 9.7 %collective-permute-start = (bf16[2,24,512]{2,1,0:T(8,128)(2,1)S(1)}, bf16[2,24,512]{2,1,0:T(8,128)(2,1)S(1)}, u32[]{:S(2)}, u32[]{:S(2)}) collective-permute-start(bf16[2,24,512]{2,1,0:T(8,128)(2,1)S(1)} %get-tuple-element.18), channel_id=1, source_target_pairs={{0,1},{2,3},{1,0},{3,2},{4,5},{6,7},{5,4},{7,6},{8,9},{10,11},{9,8... | collective-permute-start | bytes 147464 | tf_op jit(solution)/shard_map/ppermute | solution.py:426
  9.9 0.9 %copy-start = (bf16[2,128,512]{2,1,0:T(8,128)(2,1)S(1)}, bf16[2,128,512]{2,1,0:T(8,128)(2,1)}, u32[]{:S(2)}) copy-start(bf16[2,128,512]{2,1,0:T(8,128)(2,1)} %raw.3) | copy-start | bytes 786436
  10.9 0.9 %copy-start.1 = (bf16[2,128,512]{2,1,0:T(8,128)(2,1)S(1)}, bf16[2,128,512]{2,1,0:T(8,128)(2,1)}, u32[]{:S(2)}) copy-start(bf16[2,128,512]{2,1,0:T(8,128)(2,1)} %raw.3) | copy-start | bytes 786436
  11.2 14.9 %copy-start.4 = (bf16[3,3,3,256,256]{4,3,2,1,0:T(8,128)(2,1)S(1)}, bf16[3,3,3,256,256]{4,3,2,1,0:T(8,128)(2,1)}, u32[]{:S(2)}) copy-start(bf16[3,3,3,256,256]{4,3,2,1,0:T(8,128)(2,1)} %wb.1) | copy-start | bytes 10616836
  22.5 9.0 %collective-permute-start.4 = (bf16[10,5,16,128]{3,2,1,0:T(8,128)(2,1)S(1)}, bf16[10,5,16,128]{3,2,1,0:T(8,128)(2,1)S(1)}, u32[]{:S(2)}, u32[]{:S(2)}) collective-permute-start(bf16[10,5,16,128]{3,2,1,0:T(8,128)(2,1)S(1)} %get-tuple-element.13), channel_id=1, source_target_pairs={{0,24},{4,28},{8,16},{12,20},{16,8},{20,12},{24,0},{28,4},{1,25},{... | collective-permute-start | bytes 614408 | tf_op jit(solution)/shard_map/ppermute | solution.py:493
  25.0 9.1 %collective-permute-start.3 = (bf16[10,5,16,128]{3,2,1,0:T(8,128)(2,1)S(1)}, bf16[10,5,16,128]{3,2,1,0:T(8,128)(2,1)S(1)}, u32[]{:S(2)}, u32[]{:S(2)}) collective-permute-start(bf16[10,5,16,128]{3,2,1,0:T(8,128)(2,1)S(1)} %get-tuple-element.14), channel_id=1, source_target_pairs={{0,16},{4,20},{8,24},{12,28},{16,0},{20,4},{24,8},{28,12},{1,17},{... | collective-permute-start | bytes 614408 | tf_op jit(solution)/shard_map/ppermute | solution.py:493
  25.5 10.3 %copy-start.2 = (f32[256]{0:T(256)S(1)}, f32[256]{0:T(256)}, u32[]{:S(2)}) copy-start(f32[256]{0:T(256)} %param.19) | copy-start | bytes 3076
  25.5 10.3 %copy-start.3 = (f32[256]{0:T(256)S(1)}, f32[256]{0:T(256)}, u32[]{:S(2)}) copy-start(f32[256]{0:T(256)} %param.21) | copy-start | bytes 3076
  25.5 8.7 %collective-permute-start.2 = (bf16[10,5,16,128]{3,2,1,0:T(8,128)(2,1)S(1)}, bf16[10,5,16,128]{3,2,1,0:T(8,128)(2,1)S(1)}, u32[]{:S(2)}, u32[]{:S(2)}) collective-permute-start(bf16[10,5,16,128]{3,2,1,0:T(8,128)(2,1)S(1)} %get-tuple-element.15), channel_id=1, source_target_pairs={{0,8},{4,12},{8,0},{12,4},{16,24},{20,28},{24,16},{28,20},{1,9},{5... | collective-permute-start | bytes 614408 | tf_op jit(solution)/shard_map/ppermute | solution.py:493
  26.1 1.5 %copy-start.5 = (bf16[3,3,3,128,256]{4,3,2,1,0:T(8,128)(2,1)S(1)}, bf16[3,3,3,128,256]{4,3,2,1,0:T(8,128)(2,1)}, u32[]{:S(2)}) copy-start(bf16[3,3,3,128,256]{4,3,2,1,0:T(8,128)(2,1)} %wa.1) | copy-start | bytes 5308420
  29.1 5.7 %collective-permute-start.5 = (bf16[6,5,16,128]{3,2,1,0:T(8,128)(2,1)S(1)}, bf16[6,5,16,128]{3,2,1,0:T(8,128)(2,1)S(1)}, u32[]{:S(2)}, u32[]{:S(2)}) collective-permute-start(bf16[6,5,16,128]{3,2,1,0:T(8,128)(2,1)S(1)} %get-tuple-element.9), channel_id=1, source_target_pairs={{0,4},{4,0},{8,12},{12,8},{16,20},{20,16},{24,28},{28,24},{1,5},{5... | collective-permute-start | bytes 368648 | tf_op jit(solution)/shard_map/ppermute | solution.py:496
  31.5 3.3 %collective-permute-start.8 = (bf16[6,5,16,128]{3,2,1,0:T(8,128)(2,1)S(1)}, bf16[6,5,16,128]{3,2,1,0:T(8,128)(2,1)S(1)}, u32[]{:S(2)}, u32[]{:S(2)}) collective-permute-start(bf16[6,5,16,128]{3,2,1,0:T(8,128)(2,1)S(1)} %constant_dynamic-slice_fusion), channel_id=1, source_target_pairs={{0,4},{4,0},{8,12},{12,8},{16,20},{20,16},{24,28},{28,24},{1,5},{5... | collective-permute-start | bytes 368648 | tf_op jit(solution)/shard_map/ppermute | solution.py:496
  34.1 1.4 %collective-permute-start.7 = (bf16[6,5,16,128]{3,2,1,0:T(8,128)(2,1)S(1)}, bf16[6,5,16,128]{3,2,1,0:T(8,128)(2,1)S(1)}, u32[]{:S(2)}, u32[]{:S(2)}) collective-permute-start(bf16[6,5,16,128]{3,2,1,0:T(8,128)(2,1)S(1)} %constant_dynamic-slice_fusion.1), channel_id=1, source_target_pairs={{0,4},{4,0},{8,12},{12,8},{16,20},{20,16},{24,28},{28,24},{1,5},{5... | collective-permute-start | bytes 368648 | tf_op jit(solution)/shard_map/ppermute | solution.py:496
  34.3 1.5 %collective-permute-start.6 = (bf16[6,5,16,128]{3,2,1,0:T(8,128)(2,1)S(1)}, bf16[6,5,16,128]{3,2,1,0:T(8,128)(2,1)S(1)}, u32[]{:S(2)}, u32[]{:S(2)}) collective-permute-start(bf16[6,5,16,128]{3,2,1,0:T(8,128)(2,1)S(1)} %constant_dynamic-slice_fusion.2), channel_id=1, source_target_pairs={{0,4},{4,0},{8,12},{12,8},{16,20},{20,16},{24,28},{28,24},{1,5},{5... | collective-permute-start | bytes 368648 | tf_op jit(solution)/shard_map/ppermute | solution.py:496
